TPU v7x, 32 devices: a whole 2x2x4 slice. The times are simulated.
32 devices in a mesh: stream: 8 (over z, y), rep: 4 (over x, core).
Axes of the slice: x: 2, y: 2, z: 4, core: 2. Of those that a mesh axis runs over, the one named last changes fastest.
Arguments:
- queries: bfloat16 [4, 1024, 768], P('rep', 'stream'), may hold values from -6 to 6
- memory: bfloat16 [4, 8192, 768], P('rep', 'stream'), may hold values from -6 to 6
- routes: int32 [4, 64], P('rep', 'stream'), may hold values from 0 to 7, as said below
- w_self: bfloat16 [768, 2304], replicated, may hold values from -0.21875 to 0.21875
- w_self_out: bfloat16 [768, 768], replicated, may hold values from -2.5 to 2.5
- w_cross_q: bfloat16 [768, 768], replicated, may hold values from -0.21875 to 0.21875
- w_cross_kv: bfloat16 [768, 1536], replicated, may hold values from -0.21875 to 0.21875
- w_cross_out: bfloat16 [768, 768], replicated, may hold values from -3.5 to 3.5
- w_up: bfloat16 [768, 3072], replicated, may hold values from -0.21875 to 0.21875
- b_up: bfloat16 [3072], replicated, may hold values from -1.5 to 1.5
- w_down: bfloat16 [3072, 768], replicated, may hold values from -0.109375 to 0.109375
- b_down: bfloat16 [768], replicated, may hold values from -1.5 to 1.5
- gain_one: bfloat16 [768], replicated, may hold values from 0.5 to 1.5
- shift_one: bfloat16 [768], replicated, may hold values from -1.5 to 1.5
- gain_two: bfloat16 [768], replicated, may hold values from 0.5 to 1.5
- shift_two: bfloat16 [768], replicated, may hold values from -1.5 to 1.5
- gain_three: bfloat16 [768], replicated, may hold values from 0.5 to 1.5
- shift_three: bfloat16 [768], replicated, may hold values from -1.5 to 1.5
- cotangent: bfloat16 [4, 1024, 768], P('rep', 'stream'), may hold values from -6 to 6
Outputs:
- layer_out: bfloat16 [4, 1024, 768], P('rep', 'stream')
- d_queries: float32 [4, 1024, 768], P('rep', 'stream')
- d_memory: bfloat16 [4, 8192, 768], P('rep', 'stream')
- d_w_self: float32 [768, 2304], P('stream')
- d_w_self_out: float32 [768, 768], P('stream')
- d_w_cross_q: float32 [768, 768], P('stream')
- d_w_cross_kv: float32 [768, 1536], P('stream')
- d_w_cross_out: float32 [768, 768], P('stream')
- d_w_up: float32 [768, 3072], P('stream')
- d_b_up: float32 [3072], P('stream')
- d_w_down: float32 [3072, 768], P('stream')
- d_b_down: float32 [768], P('stream')
- d_gain_one: float32 [768], P('stream')
- d_shift_one: float32 [768], P('stream')
- d_gain_two: float32 [768], P('stream')
- d_shift_two: float32 [768], P('stream')
- d_gain_three: float32 [768], P('stream')
- d_shift_three: float32 [768], P('stream')
Inputs may be any that keep to these rules, and one draw needn't show every extreme that they name: `routes`: of the 8 blocks of one device, exactly 2 are read by the group of the same index of stream in the same replica, and at most 2 by any one group.
All inputs are finite; a program needn't handle non-finite values.
Results may differ from a plain program's by a relative error of at most 0.025.
Values may be sent and summed in bfloat16 or wider, within the bound.
No kernel may reach another device: no remote copies, remote signals or barrier semaphores. Data moves between devices by JAX's collectives and lax.ppermute only.
A program may use at most 384 MiB of HBM per device.

v0:
```python
import functools

import jax
import jax.numpy as jnp
from jax import lax
from jax.experimental import pallas as pl
from jax.experimental.pallas import tpu as pltpu
from jax.sharding import PartitionSpec as P

HEADS = 12
HEAD_DIM = 64
BLK = 128


def matmul(left, right):
    return jnp.dot(left, right, preferred_element_type=jnp.float32)


def product_left(left, right):
    return lax.dot_general(
        left, right, (((0,), (0,)), ((), ())), preferred_element_type=jnp.float32
    )


def product_right(left, right):
    return lax.dot_general(
        left, right, (((1,), (1,)), ((), ())), preferred_element_type=jnp.float32
    )


def layer_norm(rows, gain, shift):
    centred = rows - jnp.mean(rows, axis=-1, keepdims=True)
    spread = jnp.mean(centred * centred, axis=-1, keepdims=True)
    return centred * lax.rsqrt(spread + 1e-05) * gain + shift


def split_heads(rows):
    return rows.reshape(rows.shape[0], HEADS, HEAD_DIM).transpose(1, 0, 2)


def join_heads(rows):
    return rows.transpose(1, 0, 2).reshape(rows.shape[1], HEADS * HEAD_DIM)


def masked_scores(query_head, key_head, key_ok):
    scores = product_right(query_head, key_head) * HEAD_DIM ** (-0.5)
    if key_ok is not None:
        scores = jnp.where(key_ok[None, :], scores, -1e30)
    return scores


def attend_forward(query, key_rows, value_rows, key_ok):

    def one_head(item):
        query_head, key_head, value_head = item
        scores = masked_scores(query_head, key_head, key_ok)
        row_max = jnp.max(scores, axis=1, keepdims=True)
        exponent = jnp.exp(scores - row_max)
        row_total = jnp.sum(exponent, axis=1, keepdims=True)
        probability = (exponent / row_total).astype(jnp.bfloat16)
        return (matmul(probability, value_head), (row_max + jnp.log(row_total))[:, 0])

    mixed, log_total = lax.map(
        one_head, (split_heads(query), split_heads(key_rows), split_heads(value_rows))
    )
    return (join_heads(mixed), log_total)


def attend_backward(query, key_rows, value_rows, key_ok, log_total, d_mixed):
    factor = HEAD_DIM ** (-0.5)

    def one_head(item):
        query_head, key_head, value_head, total_head, grad_head = item
        scores = masked_scores(query_head, key_head, key_ok)
        probability = jnp.exp(scores - total_head[:, None])
        d_prob = product_right(grad_head, value_head)
        d_scores = probability * (d_prob - jnp.sum(d_prob * probability, axis=1, keepdims=True))
        d_scores = d_scores.astype(jnp.bfloat16)
        d_query = matmul(d_scores, key_head) * factor
        d_key = product_left(d_scores, query_head) * factor
        d_value = product_left(probability.astype(jnp.bfloat16), grad_head)
        return (d_query, d_key, d_value)

    d_query, d_key, d_value = lax.map(
        one_head,
        (
            split_heads(query),
            split_heads(key_rows),
            split_heads(value_rows),
            log_total,
            split_heads(d_mixed),
        ),
    )
    return (join_heads(d_query), join_heads(d_key), join_heads(d_value))


def on_device(
    queries,
    memory,
    routes,
    w_self,
    w_self_out,
    w_cross_q,
    w_cross_kv,
    w_cross_out,
    w_up,
    b_up,
    w_down,
    b_down,
    gain_one,
    shift_one,
    gain_two,
    shift_two,
    gain_three,
    shift_three,
    cotangent,
):
    streams = lax.axis_size("stream")
    blocks = routes.shape[1]
    capacity = max(2, 2 * blocks // streams)
    slot_count = streams * capacity
    model_width = w_self_out.shape[0]
    target = routes[0]
    hit_table = (target[:, None] == jnp.arange(streams, dtype=jnp.int32)[None, :]).astype(jnp.int32)
    before = jnp.cumsum(hit_table, axis=0) - hit_table
    rank_in = jnp.sum(before * hit_table, axis=1)
    slot_of_block = target * capacity + rank_in
    matched = (slot_of_block[None, :] == jnp.arange(slot_count, dtype=jnp.int32)[:, None]).astype(
        jnp.int32
    )
    block_at = jnp.sum(matched * jnp.arange(blocks, dtype=jnp.int32)[None, :], axis=1)
    live_slot = jnp.sum(matched, axis=1)
    live_grid = live_slot.reshape(streams, capacity)
    filled = (live_slot > 0)[:, None, None]
    nothing = jnp.zeros((), jnp.bfloat16)
    memory_rows = memory[0]
    projected = (
        matmul(memory_rows, w_cross_kv).astype(jnp.bfloat16).reshape(blocks, BLK, 2 * model_width)
    )
    outgoing = jnp.where(filled, jnp.take(projected, block_at, axis=0), nothing)
    arrived, arrived_live = (
        lax.all_to_all(
            outgoing.reshape(streams, capacity, BLK, 2 * model_width),
            "stream",
            split_axis=0,
            concat_axis=0,
            tiled=True,
        ),
        lax.all_to_all(live_grid, "stream", split_axis=0, concat_axis=0, tiled=True),
    )
    keys_values = arrived.reshape(-1, 2 * model_width)
    key_ok = jnp.repeat(arrived_live.reshape(-1), BLK) > 0
    key_cross = keys_values[:, :model_width]
    value_cross = keys_values[:, model_width:]
    gain_a = gain_one.astype(jnp.float32)
    shift_a = shift_one.astype(jnp.float32)
    gain_b = gain_two.astype(jnp.float32)
    shift_b = shift_two.astype(jnp.float32)
    gain_c = gain_three.astype(jnp.float32)
    shift_c = shift_three.astype(jnp.float32)
    tokens = queries[0]
    joined = matmul(tokens, w_self).astype(jnp.bfloat16)
    query_self = joined[:, :model_width]
    key_self = joined[:, model_width : 2 * model_width]
    value_self = joined[:, 2 * model_width :]
    mixed_self, total_self = attend_forward(query_self, key_self, value_self, None)
    mixed_self = mixed_self.astype(jnp.bfloat16)
    residual_one = tokens.astype(jnp.float32) + matmul(mixed_self, w_self_out)
    normed_one = layer_norm(residual_one, gain_a, shift_a).astype(jnp.bfloat16)
    query_cross = matmul(normed_one, w_cross_q).astype(jnp.bfloat16)
    mixed_cross, total_cross = attend_forward(query_cross, key_cross, value_cross, key_ok)
    mixed_cross = mixed_cross.astype(jnp.bfloat16)
    residual_two = normed_one.astype(jnp.float32) + matmul(mixed_cross, w_cross_out)
    normed_two = layer_norm(residual_two, gain_b, shift_b).astype(jnp.bfloat16)
    hidden_pre = matmul(normed_two, w_up) + b_up.astype(jnp.float32)
    hidden = jax.nn.gelu(hidden_pre, approximate=False).astype(jnp.bfloat16)
    residual_three = (
        normed_two.astype(jnp.float32) + matmul(hidden, w_down) + b_down.astype(jnp.float32)
    )
    layer_out = layer_norm(residual_three, gain_c, shift_c).astype(jnp.bfloat16)
    grad_out = cotangent[0].astype(jnp.float32)
    norm_three_pull = jax.vjp(layer_norm, residual_three, gain_c, shift_c)[1]
    d_residual_three, d_gain_c, d_shift_c = norm_three_pull(grad_out)
    d_branch_three = d_residual_three.astype(jnp.bfloat16)
    d_b_down = jnp.sum(d_branch_three.astype(jnp.float32), axis=0)
    d_w_down = product_left(hidden, d_branch_three)
    d_hidden = product_right(d_branch_three, w_down)
    gelu_pull = jax.vjp(lambda value: jax.nn.gelu(value, approximate=False), hidden_pre)[1]
    d_hidden_pre = gelu_pull(d_hidden)[0].astype(jnp.bfloat16)
    d_b_up = jnp.sum(d_hidden_pre.astype(jnp.float32), axis=0)
    d_w_up = product_left(normed_two, d_hidden_pre)
    d_normed_two = d_residual_three + product_right(d_hidden_pre, w_up)
    norm_two_pull = jax.vjp(layer_norm, residual_two, gain_b, shift_b)[1]
    d_residual_two, d_gain_b, d_shift_b = norm_two_pull(d_normed_two)
    d_branch_two = d_residual_two.astype(jnp.bfloat16)
    d_w_cross_out = product_left(mixed_cross, d_branch_two)
    d_mixed_cross = product_right(d_branch_two, w_cross_out).astype(jnp.bfloat16)
    d_query_cross, d_key_cross, d_value_cross = attend_backward(
        query_cross, key_cross, value_cross, key_ok, total_cross, d_mixed_cross
    )
    d_query_cross = d_query_cross.astype(jnp.bfloat16)
    d_keys_values = jnp.concatenate([d_key_cross, d_value_cross], axis=1).astype(jnp.bfloat16)
    d_w_cross_q = product_left(normed_one, d_query_cross)
    d_normed_one = d_residual_two + product_right(d_query_cross, w_cross_q)
    norm_one_pull = jax.vjp(layer_norm, residual_one, gain_a, shift_a)[1]
    d_residual_one, d_gain_a, d_shift_a = norm_one_pull(d_normed_one)
    d_branch_one = d_residual_one.astype(jnp.bfloat16)
    d_w_self_out = product_left(mixed_self, d_branch_one)
    d_mixed_self = product_right(d_branch_one, w_self_out).astype(jnp.bfloat16)
    d_query_self, d_key_self, d_value_self = attend_backward(
        query_self, key_self, value_self, None, total_self, d_mixed_self
    )
    d_joined = jnp.concatenate([d_query_self, d_key_self, d_value_self], axis=1).astype(
        jnp.bfloat16
    )
    d_w_self = product_left(tokens, d_joined)
    d_tokens = d_residual_one + product_right(d_joined, w_self)
    returned = lax.all_to_all(
        d_keys_values.reshape(streams, capacity, BLK, 2 * model_width),
        "stream",
        split_axis=0,
        concat_axis=0,
        tiled=True,
    )
    d_block_rows = jnp.take(
        returned.reshape(slot_count, BLK, 2 * model_width), slot_of_block, axis=0
    ).reshape(-1, 2 * model_width)
    d_w_cross_kv = product_left(memory_rows, d_block_rows)
    d_memory = product_right(d_block_rows, w_cross_kv).astype(jnp.bfloat16)
    gradients = (
        d_w_self,
        d_w_self_out,
        d_w_cross_q,
        d_w_cross_kv,
        d_w_cross_out,
        d_w_up,
        d_b_up,
        d_w_down,
        d_b_down,
        d_gain_a,
        d_shift_a,
        d_gain_b,
        d_shift_b,
        d_gain_c,
        d_shift_c,
    )
    shapes = [item.shape for item in gradients]
    flat = [item.reshape(-1) for item in gradients]
    (
        share_self,
        share_self_out,
        share_cross_q,
        share_cross_kv,
        share_cross_out,
        share_up,
        share_b_up,
        share_down,
        share_b_down,
        share_gain_a,
        share_shift_a,
        share_gain_b,
        share_shift_b,
        share_gain_c,
        share_shift_c,
    ) = (
        lax.psum_scatter(flat[0], "stream", scatter_dimension=0, tiled=True),
        lax.psum_scatter(flat[1], "stream", scatter_dimension=0, tiled=True),
        lax.psum_scatter(flat[2], "stream", scatter_dimension=0, tiled=True),
        lax.psum_scatter(flat[3], "stream", scatter_dimension=0, tiled=True),
        lax.psum_scatter(flat[4], "stream", scatter_dimension=0, tiled=True),
        lax.psum_scatter(flat[5], "stream", scatter_dimension=0, tiled=True),
        lax.psum_scatter(flat[6], "stream", scatter_dimension=0, tiled=True),
        lax.psum_scatter(flat[7], "stream", scatter_dimension=0, tiled=True),
        lax.psum_scatter(flat[8], "stream", scatter_dimension=0, tiled=True),
        lax.psum_scatter(flat[9], "stream", scatter_dimension=0, tiled=True),
        lax.psum_scatter(flat[10], "stream", scatter_dimension=0, tiled=True),
        lax.psum_scatter(flat[11], "stream", scatter_dimension=0, tiled=True),
        lax.psum_scatter(flat[12], "stream", scatter_dimension=0, tiled=True),
        lax.psum_scatter(flat[13], "stream", scatter_dimension=0, tiled=True),
        lax.psum_scatter(flat[14], "stream", scatter_dimension=0, tiled=True),
    )
    summed = (
        lax.psum(share_self.astype(jnp.bfloat16), "rep").astype(jnp.float32),
        lax.psum(share_self_out.astype(jnp.bfloat16), "rep").astype(jnp.float32),
        lax.psum(share_cross_q.astype(jnp.bfloat16), "rep").astype(jnp.float32),
        lax.psum(share_cross_kv.astype(jnp.bfloat16), "rep").astype(jnp.float32),
        lax.psum(share_cross_out.astype(jnp.bfloat16), "rep").astype(jnp.float32),
        lax.psum(share_up.astype(jnp.bfloat16), "rep").astype(jnp.float32),
        lax.psum(share_b_up.astype(jnp.bfloat16), "rep").astype(jnp.float32),
        lax.psum(share_down.astype(jnp.bfloat16), "rep").astype(jnp.float32),
        lax.psum(share_b_down.astype(jnp.bfloat16), "rep").astype(jnp.float32),
        lax.psum(share_gain_a.astype(jnp.bfloat16), "rep").astype(jnp.float32),
        lax.psum(share_shift_a.astype(jnp.bfloat16), "rep").astype(jnp.float32),
        lax.psum(share_gain_b.astype(jnp.bfloat16), "rep").astype(jnp.float32),
        lax.psum(share_shift_b.astype(jnp.bfloat16), "rep").astype(jnp.float32),
        lax.psum(share_gain_c.astype(jnp.bfloat16), "rep").astype(jnp.float32),
        lax.psum(share_shift_c.astype(jnp.bfloat16), "rep").astype(jnp.float32),
    )
    results = [
        part.reshape((shape[0] // streams,) + tuple(shape[1:]))
        for part, shape in zip(summed, shapes)
    ]
    return (
        layer_out[None],
        d_tokens[None],
        d_memory[None],
        results[0],
        results[1],
        results[2],
        results[3],
        results[4],
        results[5],
        results[6],
        results[7],
        results[8],
        results[9],
        results[10],
        results[11],
        results[12],
        results[13],
        results[14],
    )


PAIRS = HEADS // 2
LANES = 2 * HEAD_DIM
FACTOR = HEAD_DIM ** (-0.5)
BF = jnp.bfloat16
F32 = jnp.float32
AXES = ("stream", "rep")


def whole_in_vmem(count):
    return [pl.BlockSpec(memory_space=pltpu.VMEM)] * count


def local_kernel(body, out_shape, scalars=(), arrays=(), scratch=(), cost=2, limit=24):
    return pl.pallas_call(
        body,
        out_shape=list(out_shape),
        in_specs=[pl.BlockSpec(memory_space=pltpu.SMEM)] * len(scalars) + whole_in_vmem(len(arrays)),
        out_specs=whole_in_vmem(len(out_shape)),
        scratch_shapes=list(scratch),
        compiler_params=pltpu.CompilerParams(vmem_limit_bytes=limit * 1024 * 1024),
        cost_estimate=pl.CostEstimate(
            flops=int(cost * 1.15e9), bytes_accessed=int(cost * 1e5), transcendentals=0
        ),
    )(*scalars, *arrays)


def like(shape, dtype):
    return jax.ShapeDtypeStruct(shape, dtype)


def dot_nn(left, right):
    return lax.dot_general(left, right, (((1,), (0,)), ((), ())), preferred_element_type=F32)


def dot_nt(left, right):
    return lax.dot_general(left, right, (((1,), (1,)), ((), ())), preferred_element_type=F32)


def head_masks(rows):
    lane = lax.broadcasted_iota(jnp.int32, (rows, LANES), 1)
    return lane < HEAD_DIM


def stack_heads(pair, first, scale):
    one = jnp.where(first, scale, 0.0).astype(BF)
    two = jnp.where(first, 0.0, scale).astype(BF)
    return jnp.concatenate([pair * one, pair * two], axis=0)


def unstack_heads(both, first):
    rows = both.shape[0] // 2
    return jnp.where(first, both[:rows], both[rows:])


def norm_parts(rows):
    centred = rows - jnp.mean(rows, axis=1, keepdims=True)
    spread = jnp.mean(centred * centred, axis=1, keepdims=True)
    inverse = lax.rsqrt(spread + 1e-05)
    return centred * inverse, inverse


def norm_pull(grad, hat, inverse, gain):
    scaled = grad * gain
    inner = scaled - jnp.mean(scaled, axis=1, keepdims=True)
    inner = inner - hat * jnp.mean(scaled * hat, axis=1, keepdims=True)
    return (
        inverse * inner,
        jnp.sum(grad * hat, axis=0, keepdims=True),
        jnp.sum(grad, axis=0, keepdims=True),
    )


def deal_blocks(routes_ref, memory_ref, out_ref):
    out_ref[...] = jnp.zeros_like(out_ref)
    blocks = memory_ref.shape[0] // BLK
    for b in range(blocks):
        group = routes_ref[0, b]
        rank = jnp.int32(0)
        for earlier in range(b):
            rank = rank + (routes_ref[0, earlier] == group).astype(jnp.int32)
        row = pl.multiple_of(rank * BLK, BLK)
        out_ref[group, pl.ds(row, BLK), :] = memory_ref[b * BLK : (b + 1) * BLK, :]


def self_forward(tok, w_in, w_out, w_q, gain, shift, joined, r1, h1_out, qc, turned):
    width = tok.shape[1]
    rows = tok.shape[0]
    joined[...] = dot_nn(tok[...], w_in[...]).astype(BF)
    first = head_masks(rows)
    mixed = []
    for j in range(PAIRS):
        at = j * LANES
        q2 = stack_heads(joined[:, at : at + LANES], first, FACTOR)
        key = joined[:, width + at : width + at + LANES]
        value = joined[:, 2 * width + at : 2 * width + at + LANES]
        scores = dot_nt(q2, key)
        power = jnp.exp(scores - jnp.max(scores, axis=1, keepdims=True))
        prob = (power / jnp.sum(power, axis=1, keepdims=True)).astype(BF)
        mixed.append(unstack_heads(dot_nn(prob, value), first).astype(BF))
    o1 = jnp.concatenate(mixed, axis=1)
    res = tok[...].astype(F32) + dot_nn(o1, w_out[...])
    r1[...] = res
    hat, _ = norm_parts(res)
    h1 = (hat * gain[...].astype(F32) + shift[...].astype(F32)).astype(BF)
    h1_out[...] = h1
    qc[...] = dot_nn(h1, w_q[...]).astype(BF)
    turned[0:width, :] = tok[...].T
    turned[width : 2 * width, :] = o1.T
    turned[2 * width : 3 * width, :] = h1.T


def cross_forward(routes_ref, me_ref, qc, parcels, w_kv, o2, kv, sums, bias_ref, s_ref, p_ref):
    width = qc.shape[1]
    rows = qc.shape[0]
    sources = parcels.shape[0]
    span = 2 * BLK
    first = head_masks(rows)
    for k in range(sources):
        kv[k * span : (k + 1) * span, :] = dot_nn(parcels[k, 0:span, :], w_kv[...]).astype(BF)
        count = jnp.int32(0)
        for b in range(routes_ref.shape[1]):
            count = count + (routes_ref[k, b] == me_ref[0]).astype(jnp.int32)
        for c in range(2):
            bias_ref[:, k * span + c * BLK : k * span + (c + 1) * BLK] = jnp.full(
                (8, BLK), jnp.where(count > c, 0.0, -1e30), F32
            )
    lane = lax.broadcasted_iota(jnp.int32, (2 * rows, LANES), 1)
    sums[...] = jnp.zeros_like(sums)

    def one_pair(j, carry):
        at = pl.multiple_of(j * LANES, LANES)
        q2 = stack_heads(qc[:, pl.ds(at, LANES)], first, FACTOR)
        top = None
        for k in range(sources):
            key = kv[k * span : (k + 1) * span, pl.ds(at, LANES)]
            scores = dot_nt(q2, key) + bias_ref[0:1, k * span : (k + 1) * span]
            s_ref[:, k * span : (k + 1) * span] = scores
            most = jnp.maximum(scores[:, :LANES], scores[:, LANES:])
            top = most if top is None else jnp.maximum(top, most)
        peak = jnp.max(top, axis=1, keepdims=True)
        total = None
        for k in range(sources):
            power = jnp.exp(s_ref[:, k * span : (k + 1) * span] - peak)
            p_ref[:, k * span : (k + 1) * span] = power.astype(BF)
            part = power[:, :LANES] + power[:, LANES:]
            total = part if total is None else total + part
        total = jnp.sum(total, axis=1, keepdims=True)
        value = kv[:, pl.ds(pl.multiple_of(width + j * LANES, LANES), LANES)]
        both = dot_nn(p_ref[...], value) / total
        o2[:, pl.ds(at, LANES)] = unstack_heads(both, first).astype(BF)
        sums[...] = jnp.where(lane == j, peak + jnp.log(total), sums[...])
        return carry

    lax.fori_loop(0, PAIRS, one_pair, 0, unroll=PAIRS)


def feed_forward(
    rep_ref, o2, tok_h1, sums, w_co, w_up, w_down, b_up, b_down, vec, cot,
    layer_out, dr2, do2, both_sums, small, small_up, parcel0, parcel1, parcel2,
    slope, acts, dus,
):
    width = o2.shape[1]
    rows = o2.shape[0]
    hidden = w_up.shape[1]
    quarter = hidden // 4
    rep = rep_ref[0]
    gain2, shift2, gain3, shift3 = (vec[i : i + 1, :].astype(F32) for i in range(4))
    res2 = tok_h1[...].astype(F32) + dot_nn(o2[...], w_co[...])
    hat2, inv2 = norm_parts(res2)
    h2 = (hat2 * gain2 + shift2).astype(BF)
    each = 2 * quarter + width // 4
    for parcel, base in ((parcel1, 0), (parcel2, each)):
        parcel[base : base + width, :] = h2.T
        parcel[base + width : base + 2 * width, :] = o2[...].T
    total = None
    for c in range(4):
        cols = slice(c * quarter, (c + 1) * quarter)
        u = dot_nn(h2, w_up[:, cols]) + b_up[:, cols].astype(F32)
        cdf = 0.5 + 0.5 * lax.erf(u * 0.7071067811865476)
        act = (u * cdf).astype(BF)
        slope[:, cols] = cdf + u * (jnp.exp(u * u * -0.5) * 0.3989422804014327)
        acts[cols, :] = act.T
        part = dot_nn(act, w_down[cols, :])
        total = part if total is None else total + part
    res3 = h2.astype(F32) + total + b_down[...].astype(F32)
    hat3, inv3 = norm_parts(res3)
    layer_out[...] = (hat3 * gain3 + shift3).astype(BF)
    dr3, d_gain3, d_shift3 = norm_pull(cot[...].astype(F32), hat3, inv3, gain3)
    dy3 = dr3.astype(BF)
    small[0:1, :] = jnp.sum(dy3.astype(F32), axis=0, keepdims=True)
    small[3:4, :] = d_gain3
    small[4:5, :] = d_shift3
    back = None
    for c in range(4):
        cols = slice(c * quarter, (c + 1) * quarter)
        du = (dot_nt(dy3, w_down[cols, :]) * slope[:, cols]).astype(BF)
        small_up[:, cols] = jnp.sum(du.astype(F32), axis=0, keepdims=True)
        dus[cols, :] = du.T
        part = dot_nt(du, w_up[:, cols])
        back = part if back is None else back + part
    grad2, d_gain2, d_shift2 = norm_pull(dr3 + back, hat2, inv2, gain2)
    small[1:2, :] = d_gain2
    small[2:3, :] = d_shift2
    small[5:8, :] = jnp.zeros((3, width), F32)
    dr2[...] = grad2
    dy2 = grad2.astype(BF)
    grad_mixed = dot_nt(dy2, w_co[...]).astype(BF)
    do2[0:rows, :] = grad_mixed
    lane = lax.broadcasted_iota(jnp.int32, (2 * rows, LANES), 1)
    first = head_masks(rows)
    packed = sums[...]
    for j in range(PAIRS):
        at = slice(j * LANES, (j + 1) * LANES)
        prod = grad_mixed[:, at].astype(F32) * o2[:, at].astype(F32)
        zero = jnp.zeros_like(prod)
        two = jnp.concatenate([jnp.where(first, prod, zero), jnp.where(first, zero, prod)], axis=0)
        packed = jnp.where(lane == 8 + j, jnp.sum(two, axis=1, keepdims=True), packed)
    both_sums[...] = packed
    turned = packed.T[0:16, :]
    high = turned.astype(BF)
    rest = turned - high.astype(F32)
    middle = rest.astype(BF)
    low = (rest - middle.astype(F32)).astype(BF)
    do2[rows : rows + 16, :] = jnp.concatenate([high, middle, low], axis=1)
    share = width // 4
    dy2_turned = dy2.T
    dy3_turned = dy3.T
    strip = quarter // 8
    parcel1[2 * width : 3 * width, :] = dy3_turned
    parcel2[each + 2 * width : each + 3 * width, :] = dy3_turned
    places = ((parcel0, 0), (parcel1, 3 * width), (parcel2, 0), (parcel2, each + 3 * width))
    for k, (parcel, base) in enumerate(places):
        peer = rep ^ k
        for s in range(8):
            row = pl.multiple_of(s * 4 * strip + peer * strip, strip)
            parcel[base + s * strip : base + (s + 1) * strip, :] = acts[pl.ds(row, strip), :]
        row = pl.multiple_of(peer * quarter, quarter)
        parcel[base + quarter : base + 2 * quarter, :] = dus[pl.ds(row, quarter), :]
        piece = dy2_turned[0:share]
        for i in range(1, 4):
            piece = jnp.where(peer == i, dy2_turned[i * share : (i + 1) * share], piece)
        parcel[base + 2 * quarter : base + 2 * quarter + share, :] = piece


def cross_backward(qc, do2, kv, bias_ref, sums, dqc):
    width = qc.shape[1]
    rows = qc.shape[0]
    span = 2 * BLK
    sources = kv.shape[0] // span
    first = head_masks(rows)
    lane = lax.broadcasted_iota(jnp.int32, (2 * rows, LANES), 1)

    def one_pair(j, carry):
        at = pl.multiple_of(j * LANES, LANES)
        q2 = stack_heads(qc[:, pl.ds(at, LANES)], first, FACTOR)
        g2 = stack_heads(do2[0:rows, pl.ds(at, LANES)], first, 1.0)
        packed = sums[...]
        log_sum = jnp.sum(jnp.where(lane == j, packed, 0.0), axis=1, keepdims=True)
        delta = jnp.sum(jnp.where(lane == j + 8, packed, 0.0), axis=1, keepdims=True)
        total = None
        for k in range(sources):
            key = kv[k * span : (k + 1) * span, pl.ds(at, LANES)]
            value = kv[
                k * span : (k + 1) * span, pl.ds(pl.multiple_of(width + j * LANES, LANES), LANES)
            ]
            scores = dot_nt(q2, key) + bias_ref[0:1, k * span : (k + 1) * span]
            prob = jnp.exp(scores - log_sum)
            grad = (prob * (dot_nt(g2, value) - delta)).astype(BF)
            part = dot_nn(grad, key)
            total = part if total is None else total + part
        dqc[:, pl.ds(at, LANES)] = (unstack_heads(total, first) * FACTOR).astype(BF)
        return carry

    lax.fori_loop(0, PAIRS, one_pair, 0, unroll=PAIRS)


def self_backward(
    rep_ref, dqc_ref, dr2, r1, joined, w_q, w_out, w_in, gain,
    d_tok, small, out0, out1, out2, out3,
    da_ref, quarters,
):
    rows, width = dqc_ref.shape
    rep = rep_ref[0]
    first = head_masks(rows)
    dqc = dqc_ref[...]
    grad1 = dr2[...] + dot_nt(dqc, w_q[...])
    hat1, inv1 = norm_parts(r1[...])
    dr1, d_gain1, d_shift1 = norm_pull(grad1, hat1, inv1, gain[...].astype(F32))
    small[0:1, :] = d_gain1
    small[1:2, :] = d_shift1
    small[2:8, :] = jnp.zeros((6, width), F32)
    dy1 = dr1.astype(BF)
    do1 = dot_nt(dy1, w_out[...]).astype(BF)
    for j in range(PAIRS):
        at = slice(j * LANES, (j + 1) * LANES)
        key_at = slice(width + j * LANES, width + (j + 1) * LANES)
        value_at = slice(2 * width + j * LANES, 2 * width + (j + 1) * LANES)
        q2 = stack_heads(joined[:, at], first, FACTOR)
        g2 = stack_heads(do1[:, at], first, 1.0)
        key, value = joined[:, key_at], joined[:, value_at]
        scores = dot_nt(q2, key)
        power = jnp.exp(scores - jnp.max(scores, axis=1, keepdims=True))
        prob = power / jnp.sum(power, axis=1, keepdims=True)
        d_prob = dot_nt(g2, value)
        d_scores = (prob * (d_prob - jnp.sum(d_prob * prob, axis=1, keepdims=True))).astype(BF)
        da_ref[:, at] = (unstack_heads(dot_nn(d_scores, key), first) * FACTOR).astype(BF)
        da_ref[:, key_at] = product_left(d_scores, q2).astype(BF)
        da_ref[:, value_at] = product_left(prob.astype(BF), g2).astype(BF)
    d_tok[...] = dr1 + dot_nt(da_ref[...], w_in[...])
    third = 3 * width // 4
    share = width // 4
    da = da_ref[...]
    for i in range(4):
        quarters[i, :, 0:third] = da[:, i * third : (i + 1) * third]
        quarters[i, :, third : third + share] = dy1[:, i * share : (i + 1) * share]
        quarters[i, :, width : width + share] = dqc[:, i * share : (i + 1) * share]
    for k, out in enumerate((out0, out1, out2, out3)):
        out[...] = quarters[rep ^ k]


def owner_backward(where_ref, *refs):
    groups = 8
    qc_near, qc_far, do_near, do_far, kv, dkv, q_ref, g_ref, sum_ref = refs
    _, rows, width = qc_near.shape
    first = head_masks(rows)
    for k in range(groups):
        query = (qc_far if k % 2 else qc_near)[k // 2]
        extra = (do_far if k % 2 else do_near)[k // 2]
        sums = extra[rows : rows + 16, :].astype(F32)
        third = width // 3
        sum_ref[k] = sums[:, 0:third] + sums[:, third : 2 * third] + sums[:, 2 * third :]
        for j in range(PAIRS):
            at = slice(j * LANES, (j + 1) * LANES)
            q_ref[k, j] = stack_heads(query[:, at], first, FACTOR)
            g_ref[k, j] = stack_heads(extra[0:rows, at], first, 1.0)
    blocks = kv.shape[0] // BLK

    def one_block(b, carry):
        group = where_ref[b]
        row = pl.multiple_of(b * BLK, BLK)
        for j in range(PAIRS):
            key_at = slice(j * LANES, (j + 1) * LANES)
            value_at = slice(width + j * LANES, width + (j + 1) * LANES)
            key = kv[pl.ds(row, BLK), key_at]
            value = kv[pl.ds(row, BLK), value_at]
            q2 = q_ref[group, j]
            g2 = g_ref[group, j]
            log_sum = sum_ref[group, j : j + 1, :]
            delta = sum_ref[group, 8 + j : 9 + j, :]
            prob = jnp.exp(dot_nt(key, q2) - log_sum)
            grad = (prob * (dot_nt(value, g2) - delta)).astype(BF)
            dkv[pl.ds(row, BLK), key_at] = dot_nn(grad, q2).astype(BF)
            dkv[pl.ds(row, BLK), value_at] = dot_nn(prob.astype(BF), g2).astype(BF)
        return carry

    lax.fori_loop(0, blocks, one_block, 0)


def memory_weights(rep_ref, dkv, memory_turned, keep, send):
    quarter = dkv.shape[1] // 4
    rep = rep_ref[0]
    for k in range(4):
        at = pl.multiple_of((rep ^ k) * quarter, LANES)
        out = (keep, send)[k % 2]
        out[k // 2] = dot_nn(memory_turned[...], dkv[:, pl.ds(at, quarter)]).astype(BF)


def memory_backward(dkv, w_kv, d_memory):
    half = dkv.shape[0] // 2
    for i in range(2):
        span = slice(i * half, (i + 1) * half)
        d_memory[span, :] = dot_nt(dkv[span, :], w_kv[...]).astype(BF)


def own_keys(memory_ref, w_kv, kv, turned):
    kv[...] = dot_nn(memory_ref[...], w_kv[...]).astype(BF)
    turned[...] = memory_ref[...].T


def weight_blocks(plan, whole, ready, extra, bits_ref, *refs):
    left_all, right_all, product = refs[-3:]
    count = 5 if whole else 4
    outs, arrays = refs[-3 - count : -3], refs[: -3 - count]
    width, depth = left_all.shape
    rows = depth // 4
    tall = width // 8

    def blocks_of(group):
        bit = bits_ref[group]
        for i in range(4):
            for out, b in ((outs[2 * group], 1 - bit), (outs[2 * group + 1], bit)):
                if group == 0:
                    yield out, i, 2 * i + b
                else:
                    yield out, i, 4 * (i // 2) + 2 * b + i % 2

    def multiply(lefts, rights, turned, cols):
        for k, ((a, row), (g, off)) in enumerate(zip(lefts, rights)):
            span = slice(k * rows, (k + 1) * rows)
            left_all[:, span] = arrays[a][row : row + width, :]
            right = arrays[g][off : off + cols, :].T if turned else arrays[g][:, off : off + cols]
            right_all[span, 0:cols] = right
        return dot_nn(left_all[...], right_all[:, 0:cols])

    for lefts, rights, turned, cols, group, to in plan:
        product[:, 0:cols] = multiply(lefts, rights, turned, cols)
        for out, i, block in blocks_of(group):
            at = pl.multiple_of(block * tall, 16)
            out[i, 0:tall, to : to + cols] = product[pl.ds(at, tall), 0:cols].astype(BF)
    if whole:
        outs[4][...] = multiply(*whole).astype(BF)
    if ready:
        source, group, to = ready
        cols = arrays[source].shape[1]
        for out, i, block in blocks_of(group):
            at = pl.multiple_of(block * tall, 16)
            out[i, 0:tall, to : to + cols] = arrays[source][pl.ds(at, tall), :]
    if extra is not None:
        for group in range(2):
            for out, i, block in blocks_of(group):
                out[i, tall:, :] = jnp.zeros_like(out[i, tall:, :])
                if group == 0:
                    out[i, tall:, 0:LANES] = arrays[extra][block].astype(BF)


def fold_two(bits_ref, kept0, got0, kept1, got1, give0, mine0, give1, mine1):
    for bit, kept, got, give, mine in (
        (bits_ref[1], kept0, got0, give0, mine0),
        (bits_ref[0], kept1, got1, give1, mine1),
    ):
        for i in range(2):
            for out, at in ((give, 2 * i + 1 - bit), (mine, 2 * i + bit)):
                out[i] = (kept[at].astype(F32) + got[at].astype(F32)).astype(BF)


def fold_high(bits_ref, *refs):
    (give, mine), arrays = refs[-2:], refs[:-2]
    bit = bits_ref[2]
    for g in range(len(arrays) // 2):
        kept, got = arrays[2 * g], arrays[2 * g + 1]
        for out, at in ((give, 1 - bit), (mine, bit)):
            out[g] = (kept[at].astype(F32) + got[at].astype(F32)).astype(BF)


def fold_one(bits_ref, kept, got, give, mine):
    bit = bits_ref[1]
    for i in range(2):
        for out, at in ((give, 2 * i + 1 - bit), (mine, 2 * i + bit)):
            out[i] = (kept[at].astype(F32) + got[at].astype(F32)).astype(BF)


def fold_last(kept, got, out):
    out[...] = (kept[...].astype(F32) + got[...].astype(F32)).astype(BF)


def fold_core(kept, got, near, far):
    near[...] = kept[0].astype(F32) + got[0].astype(F32)
    far[...] = (kept[1].astype(F32) + got[1].astype(F32)).astype(BF)


def fold_rep(bits_ref, near, got, send, keep):
    y = bits_ref[0]
    tall = send.shape[1]
    for z in range(4):
        for out, bit in ((send, 1 - y), (keep, y)):
            at = pl.multiple_of((2 * z + bit) * tall, 16)
            out[z] = (near[pl.ds(at, tall), :] + got[pl.ds(at, tall), :].astype(F32)).astype(BF)


def lay_columns(plan, rep_ref, *refs):
    pieces, outs, held = refs[0:4], refs[4:-1], refs[-1]
    rep = rep_ref[0]
    for k in range(4):
        held[k] = pieces[k][...]
    for (group, start, cols, how), out in zip(plan, outs):
        if how == "sum":
            tall = out.shape[0]
            total = None
            for k in range(4):
                part = pieces[k][group, pieces[k].shape[1] - tall :, start : start + cols].astype(F32)
                total = part if total is None else total + part
            out[...] = total
            continue
        tall = out.shape[0] if how == "side" else out.shape[0] // 4
        for q in range(4):
            part = held[rep ^ q, group, 0:tall, start : start + cols].astype(F32)
            if how == "side":
                out[:, q * cols : (q + 1) * cols] = part
            else:
                out[q * tall : (q + 1) * tall, :] = part


ORDER = ('dq', 'self', 'owner', 'ff1', 'kv0', 'rest1', 'kv1', 'ff2', 'memory', 'kv2', 'ff3', 'rest2', 'kv3', 'rest3', 'kv4', 'ff4', 'rest4', 'kv5', 'lay_ff', 'lay_rest', 'lay_kv')
BEFORE = {'cross': ('early',), 'ffn': ('qc_z',), 'self': ('qc_y', 'do_stack'), 'ff1': ('exports',)}
RELAY = ()
COSTS = {'deal': 2, 'self_forward': 5, 'own_keys': 6, 'cross': 17, 'ffn': 12, 'dq': 20, 'self': 12, 'ff1': 5, 'rest1': 5, 'owner': 12, 'kv0': 7, 'memory': 6}
LIMITS = {}


def fast_on_device(
    queries, memory, routes, w_self, w_self_out, w_cross_q, w_cross_kv, w_cross_out, w_up, b_up,
    w_down, b_down, gain_one, shift_one, gain_two, shift_two, gain_three, shift_three, cotangent,
):
    streams, reps = lax.axis_size("stream"), lax.axis_size("rep")
    me, rep = lax.axis_index("stream"), lax.axis_index("rep")
    width = w_self_out.shape[0]
    hidden = w_up.shape[1]
    quarter, share, tall = hidden // 4, width // 4, width // streams
    tokens = queries[0]
    rows = tokens.shape[0]
    memory_rows = memory[0]
    rep_scalar = rep.reshape(1).astype(jnp.int32)
    bits = jnp.stack([me % 2, (me // 2) % 2, me // 4]).astype(jnp.int32)
    row_of = lambda v: v.reshape(1, -1)
    last = []

    def after(first, *others):
        return lax.optimization_barrier((first, others))[0]

    moving = {}

    def run(name, body, outs, arrays, **more):
        held = last + [array for key in BEFORE.get(name, ()) for array in moving[key]]
        if held:
            arrays = [after(arrays[0], *held)] + list(arrays[1:])
        results = local_kernel(body, outs, arrays=arrays, cost=COSTS.get(name, 2), limit=LIMITS.get(name, 24), **more)
        last[:] = results[:1]
        return results

    def hop(array, stream_flip=0, rep_flip=0):
        pairs = [
            (s * reps + r, (s ^ stream_flip) * reps + (r ^ rep_flip))
            for s in range(streams)
            for r in range(reps)
        ]
        return lax.ppermute(array, AXES, pairs)

    def stream_along(array):
        return [hop(array, k) for k in (2, 4, 6)]

    def stream_across(array, near):
        near = jnp.stack([array] + near)
        return [near, hop(near, 1)]

    def rep_full(array):
        far = hop(array, 0, 2)
        return [array, hop(array, 0, 1), far, hop(far, 0, 1)]

    def rep_each(parts):
        return [parts[0]] + [hop(parts[k], 0, k) for k in range(1, 4)]

    (parcels_out,) = run(
        "deal",
        deal_blocks,
        [like((streams, 2 * BLK, width), BF)],
        [memory_rows],
        scalars=[routes],
    )
    parcels = lax.all_to_all(parcels_out, "stream", split_axis=0, concat_axis=0, tiled=True)
    joined, r1, h1, qc, turned1 = run(
        "self_forward",
        self_forward,
        [
            like((rows, 3 * width), BF),
            like((rows, width), F32),
            like((rows, width), BF),
            like((rows, width), BF),
            like((3 * width, rows), BF),
        ],
        [tokens, w_self, w_self_out, w_cross_q, row_of(gain_one), row_of(shift_one)],
    )
    early = rep_full(turned1)
    moving["early"] = early
    kv_own, memory_turned = run(
        "own_keys",
        own_keys,
        [like((memory_rows.shape[0], 2 * width), BF), like(memory_rows.shape[::-1], BF)],
        [memory_rows, w_cross_kv],
    )
    routes_all = lax.all_gather(
        after(routes[0], kv_own, *early), "stream", axis=0, tiled=False
    )
    keys = streams * 2 * BLK
    o2, kv, sums, bias = run(
        "cross",
        cross_forward,
        [
            like((rows, width), BF),
            like((keys, 2 * width), BF),
            like((2 * rows, LANES), F32),
            like((8, keys), F32),
        ],
        [qc, parcels, w_cross_kv],
        scalars=[routes_all, me.reshape(1).astype(jnp.int32)],
        scratch=[pltpu.VMEM((2 * rows, keys), F32), pltpu.VMEM((2 * rows, keys), BF)],
    )
    qc_near = stream_along(after(qc, parcels))
    qc_all = stream_across(qc, qc_near)
    moving["qc_z"], moving["qc_stack"], moving["qc_y"] = qc_near, qc_all[:1], qc_all[1:]

    vec = jnp.concatenate([row_of(v) for v in (gain_two, shift_two, gain_three, shift_three)])
    each = 2 * quarter + share
    layer_out, dr2, do2, sums2, small_ff, small_up, *parts = run(
        "ffn",
        feed_forward,
        [
            like((rows, width), BF),
            like((rows, width), F32),
            like((rows + 16, width), BF),
            like((2 * rows, LANES), F32),
            like((8, width), F32),
            like((1, hidden), F32),
            like((each, rows), BF),
            like((3 * width + each, rows), BF),
            like((3 * width + 2 * each, rows), BF),
        ],
        [
            o2, h1, sums, w_cross_out, w_up, w_down, row_of(b_up), row_of(b_down), vec,
            cotangent[0],
        ],
        scalars=[rep_scalar],
        scratch=[
            pltpu.VMEM((rows, hidden), F32),
            pltpu.VMEM((hidden, rows), BF),
            pltpu.VMEM((hidden, rows), BF),
        ],
    )
    near, far = hop(parts[1], 0, 1), hop(parts[2], 0, 2)
    do2_near = stream_along(do2)
    do2_all = stream_across(do2, do2_near)
    moving["do_z"], moving["do_stack"], moving["do_y"] = do2_near, do2_all[:1], do2_all[1:]
    moving["near"], moving["far"] = [near], [far]
    v = {}

    def step_dq():
        (v["dqc"],) = run(
            "dq", cross_backward, [like((rows, width), BF)], [qc, do2, kv, bias, sums2]
        )

    def step_self():
        v["d_tokens"], v["small_self"], *exports = run(
            "self",
            self_backward,
            [like((rows, width), F32), like((8, width), F32)]
            + [like((rows, width + share), BF)] * 4,
            [v["dqc"], dr2, r1, joined, w_cross_q, w_self_out, w_self, row_of(gain_one)],
            scalars=[rep_scalar],
            scratch=[
                pltpu.VMEM((rows, 3 * width), BF),
                pltpu.VMEM((4, rows, width + share), BF),
            ],
        )
        v["grads"] = rep_each(exports)
        moving["exports"] = v["grads"][1:]
        relayed = hop(after(far, v["small_self"], *[a for k in RELAY for a in moving[k]]), 0, 1)
        moving["relay"] = [relayed]
        v["shared"] = [parts[1], near, far, relayed, parts[0]]

    def full_at(row):
        return ((0, row), (1, row), (2, each + row), (3, each + row))

    def each_at(row):
        return ((4, row), (1, 3 * width + row), (2, row), (3, each + 3 * width + row))

    def blocks_of(name, plan, arrays, size, wide, whole=None, ready=None, extra=None):
        return run(
            name,
            functools.partial(weight_blocks, plan, whole, ready, extra),
            [like((4, size, wide), BF)] * 4 + ([like((width, whole[3]), BF)] if whole else []),
            arrays,
            scalars=[bits],
            scratch=[
                pltpu.VMEM((width, 4 * rows), BF),
                pltpu.VMEM((4 * rows, width), BF),
                pltpu.VMEM((width, width), F32),
            ],
        )

    def first_hops(key, blocks):
        send0, keep0, send1, keep1 = blocks
        v[key] = [keep0, hop(send0, 1), keep1, hop(send1, 2)]

    def second_hops(name, key):
        give0, mine0, give1, mine1 = run(
            name, fold_two, [like((2,) + v[key][0].shape[1:], BF)] * 4, v[key], scalars=[bits]
        )
        v[key] = [mine0, hop(give0, 2), mine1, hop(give1, 1)]

    def third_hop(name, key):
        arrays = v[key]
        give, mine = run(
            name,
            fold_high,
            [like((len(arrays) // 2,) + arrays[0].shape[1:], BF)] * 2,
            arrays,
            scalars=[bits],
        )
        v[key] = [mine, hop(give, 4)]

    def last_hops(name, key):
        (piece,) = run(name, fold_last, [like(v[key][0].shape, BF)], v[key])
        v[key] = rep_full(piece)

    def gathered(name, key, plan, shapes):
        return run(
            name,
            functools.partial(lay_columns, plan),
            [like(shape, F32) for shape in shapes],
            v[key],
            scalars=[rep_scalar],
            scratch=[pltpu.VMEM((4,) + v[key][0].shape, BF)],
        )

    def step_ff1():
        *blocks, v["cross_out"] = blocks_of(
            "ff1",
            [
                (full_at(0), each_at(quarter), True, quarter, 0, 0),
                (each_at(0), full_at(2 * width), True, width, 1, 0),
            ],
            v["shared"],
            tall,
            width,
            whole=(full_at(width), each_at(2 * quarter), True, share),
        )
        first_hops("ff", blocks)
        moving["ff_first"] = [v["ff"][1], v["ff"][3]]

    def step_rest1():
        vectors = jnp.concatenate([small_ff[0:5], v["small_self"][0:2]]).reshape(7, streams, tall)
        vectors = jnp.pad(vectors.transpose(1, 0, 2), ((0, 0), (0, 0), (0, LANES - tall)))
        vectors = jnp.concatenate(
            [
                vectors,
                small_up.reshape(streams, -1, LANES),
                jnp.zeros((streams, 9 - hidden // streams // LANES, LANES), F32),
            ],
            axis=1,
        )
        early_at = lambda row: tuple((k, row) for k in range(4))
        grads_at = lambda col: tuple((4 + k, col) for k in range(4))
        first_hops(
            "rest",
            blocks_of(
                "rest1",
                [
                    (early_at(0), grads_at(0), False, 3 * share, 0, 0),
                    (early_at(width), grads_at(3 * share), False, share, 1, 0),
                    (early_at(2 * width), grads_at(4 * share), False, share, 1, share),
                ],
                early + v["grads"] + [vectors, v["cross_out"]],
                tall + 16,
                3 * share,
                ready=(9, 1, 2 * share),
                extra=8,
            ),
        )
        moving["rest_first"] = [v["rest"][1], v["rest"][3]]

    kv_wide = 2 * width // 4

    def step_owner():
        (v["dkv"],) = run(
            "owner",
            owner_backward,
            [like((memory_rows.shape[0], 2 * width), BF)],
            qc_all + do2_all + [kv_own],
            scalars=[(routes[0] ^ me).astype(jnp.int32)],
            scratch=[
                pltpu.VMEM((streams, PAIRS, 2 * rows, LANES), BF),
                pltpu.VMEM((streams, PAIRS, 2 * rows, LANES), BF),
                pltpu.VMEM((streams, 16, 2 * rows), F32),
            ],
        )

    def step_kv0():
        kv_keep, kv_send = run(
            "kv0",
            memory_weights,
            [like((2, width, kv_wide), BF)] * 2,
            [v["dkv"], memory_turned],
            scalars=[rep_scalar],
        )
        v["kv"] = [kv_keep, hop(kv_send, 0, 1)]

    def step_kv1():
        near_sum, far_sum = run(
            "kv1", fold_core, [like((width, kv_wide), F32), like((width, kv_wide), BF)], v["kv"]
        )
        v["kv"] = [near_sum, hop(far_sum, 0, 2)]

    def step_kv2():
        send, keep = run(
            "kv2", fold_rep, [like((4, tall, kv_wide), BF)] * 2, v["kv"], scalars=[bits]
        )
        v["kv"] = [keep, hop(send, 1)]

    def step_kv3():
        give, mine = run(
            "kv3", fold_one, [like((2, tall, kv_wide), BF)] * 2, v["kv"], scalars=[bits]
        )
        v["kv"] = [mine, hop(give, 2)]

    def step_memory():
        (v["d_memory"],) = run(
            "memory", memory_backward, [like(memory_rows.shape, BF)], [v["dkv"], w_cross_kv]
        )

    def step_lay_ff():
        v["g_up"], v["g_down"] = gathered(
            "lay_ff",
            "ff",
            [(0, 0, quarter, "side"), (1, 0, width, "below")],
            [(tall, hidden), (hidden // streams, width)],
        )

    def step_lay_rest():
        v["g_self"], v["g_self_out"], v["g_query"], v["g_out"], v["g_vec"] = gathered(
            "lay_rest",
            "rest",
            [
                (0, 0, 3 * share, "side"),
                (1, 0, share, "side"),
                (1, share, share, "side"),
                (1, 2 * share, share, "side"),
                (0, 0, LANES, "sum"),
            ],
            [(tall, 3 * width), (tall, width), (tall, width), (tall, width), (16, LANES)],
        )

    def step_lay_kv():
        (v["g_kv"],) = gathered("lay_kv", "kv", [(0, 0, kv_wide, "side")], [(tall, 2 * width)])

    steps = {
        "dq": step_dq,
        "self": step_self,
        "ff1": step_ff1,
        "rest1": step_rest1,
        "owner": step_owner,
        "kv0": step_kv0,
        "kv1": step_kv1,
        "kv2": step_kv2,
        "kv3": step_kv3,
        "kv4": lambda: third_hop("kv4", "kv"),
        "kv5": lambda: last_hops("kv5", "kv"),
        "ff2": lambda: second_hops("ff2", "ff"),
        "ff3": lambda: third_hop("ff3", "ff"),
        "ff4": lambda: last_hops("ff4", "ff"),
        "rest2": lambda: second_hops("rest2", "rest"),
        "rest3": lambda: third_hop("rest3", "rest"),
        "rest4": lambda: last_hops("rest4", "rest"),
        "memory": step_memory,
        "lay_ff": step_lay_ff,
        "lay_rest": step_lay_rest,
        "lay_kv": step_lay_kv,
    }
    for name in ORDER:
        steps[name]()
    piece = lambda row: v["g_vec"][row, 0:tall]
    return (
        layer_out[None],
        v["d_tokens"][None],
        v["d_memory"][None],
        v["g_self"],
        v["g_self_out"],
        v["g_query"],
        v["g_kv"],
        v["g_out"],
        v["g_up"],
        v["g_vec"][7 : 7 + hidden // streams // LANES].reshape(-1),
        v["g_down"],
        piece(0),
        piece(5),
        piece(6),
        piece(1),
        piece(2),
        piece(3),
        piece(4),
    )


def solution(mesh):
    in_specs = (
        P("rep", "stream", None),
        P("rep", "stream", None),
        P("rep", "stream"),
        P(),
        P(),
        P(),
        P(),
        P(),
        P(),
        P(),
        P(),
        P(),
        P(),
        P(),
        P(),
        P(),
        P(),
        P(),
        P("rep", "stream", None),
    )
    out_specs = (
        P("rep", "stream", None),
        P("rep", "stream", None),
        P("rep", "stream", None),
        P("stream", None),
        P("stream", None),
        P("stream", None),
        P("stream", None),
        P("stream", None),
        P("stream", None),
        P("stream"),
        P("stream", None),
        P("stream"),
        P("stream"),
        P("stream"),
        P("stream"),
        P("stream"),
        P("stream"),
        P("stream"),
    )
    small_slice = (mesh.shape["stream"], mesh.shape["rep"]) == (8, 4)
    return jax.shard_map(
        fast_on_device if small_slice else on_device, mesh=mesh, in_specs=in_specs, out_specs=out_specs, check_vma=False
    )
```

profile of v0, /device:TPU:0, one launch (start us, length us, event | category | flops | bytes accessed | tf_op | source)
XLA Modules:
  0.0 262.5 jit_solution(11416335230479308850)
XLA Ops:
  5.2 7.4 %all-to-all-start = ((bf16[8,256,768]{2,1,0:T(8,128)(2,1)}), bf16[8,256,768]{2,1,0:T(8,128)(2,1)S(1)}, u32[]{:S(2)}, u32[]{:S(2)}) async-start(bf16[8,256,768]{2,1,0:T(8,128)(2,1)} %copy-done), calls=%async_computation | async-start | bytes 6291456 | tf_op jit(solution)/shard_map/all_to_all | solution.py:883
  12.7 2.0 copy-done.3
  17.2 3.0 %shard_map.323 = (bf16[128,2304]{1,0:T(8,128)(2,1)S(1)}, f32[128,768]{1,0:T(8,128)S(1)}, bf16[128,768]{1,0:T(8,128)(2,1)S(1)}, bf16[128,768]{1,0:T(8,128)(2,1)S(1)}, bf16[2304,128]{1,0:T(8,128)(2,1)}) custom-call(bf16[128,768]{1,0:T(8,128)(2,1)S(1)} %bitcast.47, bf16[768,2304]{1,0:T(8,128)(2,1)S(1)} %copy-done.3, bf16[768,768]{1,0:T(8,128)(2,1)S(1)} %copy-done.11, ...), custom_call_target="tpu_custom_call" | custom-call | flops 5750000128 | bytes 500000 | tf_op jit(solution)/shard_map/pallas_call | solution.py:338
  29.4 8.1 %collective-permute-done.1.refs_2_ = bf16[2304,128]{1,0:T(8,128)(2,1)} collective-permute-done((bf16[2304,128]{1,0:T(8,128)(2,1)}, bf16[2304,128]{1,0:T(8,128)(2,1)}, u32[]{:S(2)}, u32[]{:S(2)}) %collective-permute-start.1) | collective-permute-done | bytes 589856 | tf_op jit(solution)/shard_map/ppermute | solution.py:860
  40.7 2.6 shard_map.324
  47.1 36.6 %all-reduce.1 = s32[64]{0:T(128)S(1)} all-reduce(s32[64]{0:T(128)S(1)} %dynamic-update-slice), channel_id=2, replica_groups=mesh['stream'=8,'rep'=4] {'stream'}, use_global_device_ids=true, to_apply=%add.1 | all-reduce | flops 64 | bytes 512
  83.8 2.8 %collective-permute-start.4 = (bf16[128,768]{1,0:T(8,128)(2,1)S(1)}, bf16[128,768]{1,0:T(8,128)(2,1)S(1)}, u32[]{:S(2)}, u32[]{:S(2)}) collective-permute-start(bf16[128,768]{1,0:T(8,128)(2,1)S(1)} %get-tuple-element.124.qc), channel_id=1, source_target_pairs={{0,16},{1,17},{2,18},{3,19},{4,20},{5,21},{6,22},{7,23},{8,24},{9,... | collective-permute-start | bytes 589832 | tf_op jit(solution)/shard_map/ppermute | solution.py:860
  89.8 11.2 %shard_map.325 = (bf16[128,768]{1,0:T(8,128)(2,1)S(1)}, bf16[2048,1536]{1,0:T(8,128)(2,1)S(1)}, f32[256,128]{1,0:T(8,128)S(1)}, f32[8,2048]{1,0:T(8,128)S(1)}) custom-call(s32[8,8]{1,0:T(8,128)S(1)} %reshape.89.routes_ref, s32[1]{0:T(128)} %bitcast.5.me_ref, bf16[128,768]{1,0:T(8,128)(2,1)S(1)} %get-tuple-element.124.qc, ...), custom_call_target="tpu_custom_call" | custom-call | flops 19549999104 | bytes 1700000 | tf_op jit(solution)/shard_map/pallas_call | solution.py:338
  101.1 2.3 copy-done.1
  103.4 2.3 copy-done.2
  105.7 7.5 %shard_map.326 = (bf16[128,768]{1,0:T(8,128)(2,1)}, f32[128,768]{1,0:T(8,128)S(1)}, bf16[144,768]{1,0:T(8,128)(2,1)S(1)}, f32[256,128]{1,0:T(8,128)S(1)}, f32[8,...) custom-call(s32[1]{0:T(128)} %bitcast.rep_ref, ...), custom_call_target="tpu_custom_call" | custom-call | flops 13799999488 | bytes 1200000 | tf_op jit(solution)/shard_map/pallas_call | solution.py:338
  113.2 2.3 collective-permute-start.9
  115.5 2.8 %collective-permute-start.8 = (bf16[144,768]{1,0:T(8,128)(2,1)S(1)}, bf16[144,768]{1,0:T(8,128)(2,1)S(1)}, u32[]{:S(2)}, u32[]{:S(2)}) collective-permute-start(bf16[144,768]{1,0:T(8,128)(2,1)S(1)} %get-tuple-element.125.do2), channel_id=1, source_target_pairs={{0,16},{1,17},{2,18},{3,19},{4,20},{5,21},{6,22},{7,23},{8,24},{9,... | collective-permute-start | bytes 663560 | tf_op jit(solution)/shard_map/ppermute | solution.py:860
  120.8 8.9 %shard_map.327.dqc_ref = bf16[128,768]{1,0:T(8,128)(2,1)S(1)} custom-call(bf16[128,768]{1,0:T(8,128)(2,1)S(1)} %get-tuple-element.124.qc, bf16[144,768]{1,0:T(8,128)(2,1)S(1)} %get-tuple-element.125.do2, bf16[2048,1536]{1,0:T(8,128)(2,1)S(1)} %get-tuple-element.126.kv, f32[8,2048]{1,0:T(8,128)S(1)} %get-tuple-element.127.bias_ref, ...), custom_call_target="tpu_custom_call" | custom-call | flops 23000000512 | bytes 2000000 | tf_op jit(solution)/shard_map/pallas_call | solution.py:338
  129.7 4.9 %collective-permute-done.8 = bf16[144,768]{1,0:T(8,128)(2,1)S(1)} collective-permute-done((bf16[144,768]{1,0:T(8,128)(2,1)S(1)}, bf16[144,768]{1,0:T(8,128)(2,1)S(1)}, u32[]{:S(2)}, u32[]{:S(2)}) %collective-permute-start.8) | collective-permute-done | bytes 221216 | tf_op jit(solution)/shard_map/ppermute | solution.py:860
  136.7 6.5 %shard_map.328 = (f32[128,768]{1,0:T(8,128)}, f32[8,768]{1,0:T(8,128)S(1)}, bf16[128,960]{1,0:T(8,128)(2,1)S(1)}, bf16[128,960]{1,0:T(8,128)(2,1)S(1)}, bf16[128...) custom-call(s32[1]{0:T(128)} %bitcast.rep_ref, bf16[128,768]{1,0:T(8,128)(2,1)S(1)} %shard_map.327.dqc_ref, ...), custom_call_target="tpu_custom_call" | custom-call | flops 13799999488 | bytes 1200000 | tf_op jit(solution)/shard_map/pallas_call | solution.py:338
  143.9 7.9 %collective-permute-done.15.refs_2_ = bf16[5760,128]{1,0:T(8,128)(2,1)S(1)} collective-permute-done((bf16[5760,128]{1,0:T(8,128)(2,1)S(1)}, bf16[5760,128]{1,0:T(8,128)(2,1)S(1)}, u32[]{:S(2)}, u32[]{:S(2)}) %collective-permute-start.15) | collective-permute-done | bytes 1474592 | tf_op jit(solution)/shard_map/ppermute | solution.py:860
  153.8 2.1 collective-permute-done.10.refs_3_
  155.9 11.4 %shard_map.329.dkv = bf16[1024,1536]{1,0:T(8,128)(2,1)S(1)} custom-call(s32[8]{0:T(128)S(1)} %broadcast_xor_fusion.where_ref, bf16[4,128,768]{2,1,0:T(8,128)(2,1)S(1)} %pad_maximum_fusion.1.refs_0_, bf16[4,128,768]{2,1,0:T(8,128)(2,1)S(1)} %collective-permute-done.6.refs_1_, bf16[4,144,768]{2,1,0:T(8,128)(2,1)S(1)} %pad_maximum_fusion.refs_2_, ...), custom_call_target="tpu_custom_call" | custom-call | flops 13799999488 | bytes 1200000 | tf_op jit(solution)/shard_map/pallas_call | solution.py:338
  167.4 2.6 shard_map.330
  172.5 3.4 %shard_map.331 = (bf16[2,768,384]{2,1,0:T(8,128)(2,1)S(1)}, bf16[2,768,384]{2,1,0:T(8,128)(2,1)S(1)}) custom-call(s32[1]{0:T(128)} %bitcast.rep_ref, bf16[1024,1536]{1,0:T(8,128)(2,1)S(1)} %shard_map.329.dkv, bf16[768,1024]{1,0:T(8,128)(2,1)S(1)} %copy-done.38), custom_call_target="tpu_custom_call" | custom-call | flops 8049999872 | bytes 700000 | tf_op jit(solution)/shard_map/pallas_call | solution.py:338
  185.8 3.3 %shard_map.332 = (bf16[4,112,576]{2,1,0:T(8,128)(2,1)S(1)}, bf16[4,112,576]{2,1,0:T(8,128)(2,1)S(1)}, bf16[4,112,576]{2,1,0:T(8,128)(2,1)S(1)}, bf16[4,112,576]{2,1,0:T(8,128)(2,1)S(1)}) custom-call(s32[3]{0:T(128)S(1)} %pad_add_fusion.bits_ref, bf16[2304,128]{1,0:T(8,128)(2,1)} %get-tuple-element.148.refs_0_, ...), custom_call_target="tpu_custom_call" | custom-call | flops 5750000128 | bytes 500000 | tf_op jit(solution)/shard_map/pallas_call | solution.py:338
  191.7 4.8 %collective-permute-done.18.got0 = bf16[4,96,768]{2,1,0:T(8,128)(2,1)S(1)} collective-permute-done((bf16[4,96,768]{2,1,0:T(8,128)(2,1)}, bf16[4,96,768]{2,1,0:T(8,128)(2,1)S(1)}, u32[]{:S(2)}, u32[]{:S(2)}) %collective-permute-start.18) | collective-permute-done | bytes 589856 | tf_op jit(solution)/shard_map/ppermute | solution.py:860
  196.5 1.8 collective-permute-done.19.got1
  201.2 3.8 %shard_map.335 = bf16[1024,768]{1,0:T(8,128)(2,1)} custom-call(bf16[1024,1536]{1,0:T(8,128)(2,1)S(1)} %copy-done.34, bf16[768,1536]{1,0:T(8,128)(2,1)S(1)} %copy-done.7), custom_call_target="tpu_custom_call" | custom-call | flops 6899999744 | bytes 600000 | tf_op jit(solution)/shard_map/pallas_call | solution.py:338
  205.0 7.2 %collective-permute-done.20.got = bf16[768,384]{1,0:T(8,128)(2,1)S(1)} collective-permute-done((bf16[768,384]{1,0:T(8,128)(2,1)S(1)}, bf16[768,384]{1,0:T(8,128)(2,1)S(1)}, u32[]{:S(2)}, u32[]{:S(2)}) %collective-permute-start.20) | collective-permute-done | bytes 589856 | tf_op jit(solution)/shard_map/ppermute | solution.py:860
  218.7 3.3 %collective-permute-start.29 = (bf16[2,96,768]{2,1,0:T(8,128)(2,1)S(1)}, bf16[2,96,768]{2,1,0:T(8,128)(2,1)S(1)}, u32[]{:S(2)}, u32[]{:S(2)}) collective-permute-start(bf16[2,96,768]{2,1,0:T(8,128)(2,1)S(1)} %get-tuple-element.170), channel_id=1, source_target_pairs={{0,16},{1,17},{2,18},{3,19},{4,20},{5,21},{6,22},{7,23},{8,24},{9,... | collective-permute-start | bytes 884744 | tf_op jit(solution)/shard_map/ppermute | solution.py:860
  223.6 8.9 %collective-permute-done.26.refs_1_ = bf16[2,112,576]{2,1,0:T(8,128)(2,1)S(1)} collective-permute-done((bf16[2,112,576]{2,1,0:T(8,128)(2,1)S(1)}, bf16[2,112,576]{2,1,0:T(8,128)(2,1)S(1)}, u32[]{:S(2)}, u32[]{:S(2)}) %collective-permute-start.26) | collective-permute-done | bytes 258080 | tf_op jit(solution)/shard_map/ppermute | solution.py:860
  236.2 3.6 %collective-permute-start.31 = (bf16[1,96,384]{2,1,0:T(8,128)(2,1)S(1)}, bf16[1,96,384]{2,1,0:T(8,128)(2,1)S(1)}, u32[]{:S(2)}, u32[]{:S(2)}) collective-permute-start(bf16[1,96,384]{2,1,0:T(8,128)(2,1)S(1)} %get-tuple-element.187), channel_id=1, source_target_pairs={{0,16},{1,17},{2,18},{3,19},{4,20},{5,21},{6,22},{7,23},{8,24},{9,... | collective-permute-start | bytes 221192 | tf_op jit(solution)/shard_map/ppermute | solution.py:860
  239.8 8.7 %collective-permute-done.30.got = bf16[2,112,576]{2,1,0:T(8,128)(2,1)S(1)} collective-permute-done((bf16[2,112,576]{2,1,0:T(8,128)(2,1)S(1)}, bf16[2,112,576]{2,1,0:T(8,128)(2,1)S(1)}, u32[]{:S(2)}, u32[]{:S(2)}) %collective-permute-start.30) | collective-permute-done | bytes 258080 | tf_op jit(solution)/shard_map/ppermute | solution.py:860
  249.2 2.0 collective-permute-start.39
  251.2 4.7 %collective-permute-done.36.refs_2_ = bf16[2,112,576]{2,1,0:T(8,128)(2,1)S(1)} collective-permute-done((bf16[2,112,576]{2,1,0:T(8,128)(2,1)S(1)}, bf16[2,112,576]{2,1,0:T(8,128)(2,1)S(1)}, u32[]{:S(2)}, u32[]{:S(2)}) %collective-permute-start.36) | collective-permute-done | bytes 258080 | tf_op jit(solution)/shard_map/ppermute | solution.py:860
  (212 shorter events, 69.6 us)
Async XLA Ops:
  5.2 78.5 %all-to-all-start = ((bf16[8,256,768]{2,1,0:T(8,128)(2,1)}), bf16[8,256,768]{2,1,0:T(8,128)(2,1)S(1)}, u32[]{:S(2)}, u32[]{:S(2)}) async-start(bf16[8,256,768]{2,1,0:T(8,128)(2,1)} %copy-done), calls=%async_computation | async-start | bytes 6291456 | tf_op jit(solution)/shard_map/all_to_all | solution.py:883
  22.5 15.1 %collective-permute-start.1 = (bf16[2304,128]{1,0:T(8,128)(2,1)}, bf16[2304,128]{1,0:T(8,128)(2,1)}, u32[]{:S(2)}, u32[]{:S(2)}) collective-permute-start(bf16[2304,128]{1,0:T(8,128)(2,1)} %get-tuple-element.148.refs_0_), channel_id=1, source_target_pairs={{0,2},{1,3},{2,0},{3,1},{4,6},{5,7},{6,4},{7,5},{8,10},{9,11},{10,... | collective-permute-start | bytes 1769480 | tf_op jit(solution)/shard_map/ppermute | solution.py:860
  24.0 22.1 %collective-permute-start = (bf16[2304,128]{1,0:T(8,128)(2,1)}, bf16[2304,128]{1,0:T(8,128)(2,1)}, u32[]{:S(2)}, u32[]{:S(2)}) collective-permute-start(bf16[2304,128]{1,0:T(8,128)(2,1)} %get-tuple-element.148.refs_0_), channel_id=1, source_target_pairs={{0,1},{1,0},{2,3},{3,2},{4,5},{5,4},{6,7},{7,6},{8,9},{9,8},{10,11... | collective-permute-start | bytes 1769480 | tf_op jit(solution)/shard_map/ppermute | solution.py:860
  83.8 17.2 %collective-permute-start.3 = (bf16[128,768]{1,0:T(8,128)(2,1)S(1)}, bf16[128,768]{1,0:T(8,128)(2,1)S(1)}, u32[]{:S(2)}, u32[]{:S(2)}) collective-permute-start(bf16[128,768]{1,0:T(8,128)(2,1)S(1)} %get-tuple-element.124.qc), channel_id=1, source_target_pairs={{0,8},{1,9},{2,10},{3,11},{4,12},{5,13},{6,14},{7,15},{8,0},{9,1},... | collective-permute-start | bytes 589832 | tf_op jit(solution)/shard_map/ppermute | solution.py:860
  83.8 17.2 %collective-permute-start.4 = (bf16[128,768]{1,0:T(8,128)(2,1)S(1)}, bf16[128,768]{1,0:T(8,128)(2,1)S(1)}, u32[]{:S(2)}, u32[]{:S(2)}) collective-permute-start(bf16[128,768]{1,0:T(8,128)(2,1)S(1)} %get-tuple-element.124.qc), channel_id=1, source_target_pairs={{0,16},{1,17},{2,18},{3,19},{4,20},{5,21},{6,22},{7,23},{8,24},{9,... | collective-permute-start | bytes 589832 | tf_op jit(solution)/shard_map/ppermute | solution.py:860
  86.6 14.4 %collective-permute-start.5 = (bf16[128,768]{1,0:T(8,128)(2,1)S(1)}, bf16[128,768]{1,0:T(8,128)(2,1)S(1)}, u32[]{:S(2)}, u32[]{:S(2)}) collective-permute-start(bf16[128,768]{1,0:T(8,128)(2,1)S(1)} %get-tuple-element.124.qc), channel_id=1, source_target_pairs={{0,24},{1,25},{2,26},{3,27},{4,28},{5,29},{6,30},{7,31},{8,16},{9,... | collective-permute-start | bytes 589832 | tf_op jit(solution)/shard_map/ppermute | solution.py:860
  113.2 16.5 %collective-permute-start.9 = (bf16[144,768]{1,0:T(8,128)(2,1)S(1)}, bf16[144,768]{1,0:T(8,128)(2,1)S(1)}, u32[]{:S(2)}, u32[]{:S(2)}) collective-permute-start(bf16[144,768]{1,0:T(8,128)(2,1)S(1)} %get-tuple-element.125.do2), channel_id=1, source_target_pairs={{0,24},{1,25},{2,26},{3,27},{4,28},{5,29},{6,30},{7,31},{8,16},{9,... | collective-permute-start | bytes 663560 | tf_op jit(solution)/shard_map/ppermute | solution.py:860
  115.5 19.1 %collective-permute-start.8 = (bf16[144,768]{1,0:T(8,128)(2,1)S(1)}, bf16[144,768]{1,0:T(8,128)(2,1)S(1)}, u32[]{:S(2)}, u32[]{:S(2)}) collective-permute-start(bf16[144,768]{1,0:T(8,128)(2,1)S(1)} %get-tuple-element.125.do2), channel_id=1, source_target_pairs={{0,16},{1,17},{2,18},{3,19},{4,20},{5,21},{6,22},{7,23},{8,24},{9,... | collective-permute-start | bytes 663560 | tf_op jit(solution)/shard_map/ppermute | solution.py:860
  118.3 16.3 %collective-permute-start.7 = (bf16[144,768]{1,0:T(8,128)(2,1)S(1)}, bf16[144,768]{1,0:T(8,128)(2,1)S(1)}, u32[]{:S(2)}, u32[]{:S(2)}) collective-permute-start(bf16[144,768]{1,0:T(8,128)(2,1)S(1)} %get-tuple-element.125.do2), channel_id=1, source_target_pairs={{0,8},{1,9},{2,10},{3,11},{4,12},{5,13},{6,14},{7,15},{8,0},{9,1},... | collective-permute-start | bytes 663560 | tf_op jit(solution)/shard_map/ppermute | solution.py:860
  118.5 18.1 %collective-permute-start.6 = (bf16[4,128,768]{2,1,0:T(8,128)(2,1)S(1)}, bf16[4,128,768]{2,1,0:T(8,128)(2,1)S(1)}, u32[]{:S(2)}, u32[]{:S(2)}) collective-permute-start(bf16[4,128,768]{2,1,0:T(8,128)(2,1)S(1)} %pad_maximum_fusion.1.refs_0_), channel_id=1, source_target_pairs={{0,4},{1,5},{2,6},{3,7},{4,0},{5,1},{6,2},{7,3},{8,12},{9,13},{10,... | collective-permute-start | bytes 2359304 | tf_op jit(solution)/shard_map/ppermute | solution.py:860
  119.3 32.5 %collective-permute-start.15 = (bf16[5760,128]{1,0:T(8,128)(2,1)S(1)}, bf16[5760,128]{1,0:T(8,128)(2,1)S(1)}, u32[]{:S(2)}, u32[]{:S(2)}) collective-permute-start(bf16[5760,128]{1,0:T(8,128)(2,1)S(1)} %get-tuple-element.139), channel_id=1, source_target_pairs={{0,2},{1,3},{2,0},{3,1},{4,6},{5,7},{6,4},{7,5},{8,10},{9,11},{10,... | collective-permute-start | bytes 4423688 | tf_op jit(solution)/shard_map/ppermute | solution.py:860
  134.8 21.1 %collective-permute-start.10 = (bf16[4,144,768]{2,1,0:T(8,128)(2,1)S(1)}, bf16[4,144,768]{2,1,0:T(8,128)(2,1)S(1)}, u32[]{:S(2)}, u32[]{:S(2)}) collective-permute-start(bf16[4,144,768]{2,1,0:T(8,128)(2,1)S(1)} %pad_maximum_fusion.refs_2_), channel_id=1, source_target_pairs={{0,4},{1,5},{2,6},{3,7},{4,0},{5,1},{6,2},{7,3},{8,12},{9,13},{10,... | collective-permute-start | bytes 2654216 | tf_op jit(solution)/shard_map/ppermute | solution.py:860
  151.7 15.6 %collective-permute-start.16 = (bf16[5760,128]{1,0:T(8,128)(2,1)S(1)}, bf16[5760,128]{1,0:T(8,128)(2,1)S(1)}, u32[]{:S(2)}, u32[]{:S(2)}) collective-permute-start(bf16[5760,128]{1,0:T(8,128)(2,1)S(1)} %collective-permute-done.15.refs_2_), channel_id=1, source_target_pairs={{0,1},{1,0},{2,3},{3,2},{4,5},{5,4},{6,7},{7,6},{8,9},{9,8},{10,11... | collective-permute-start | bytes 4423688 | tf_op jit(solution)/shard_map/ppermute | solution.py:860
  151.8 15.6 %collective-permute-start.14 = (bf16[4032,128]{1,0:T(8,128)(2,1)S(1)}, bf16[4032,128]{1,0:T(8,128)(2,1)S(1)}, u32[]{:S(2)}, u32[]{:S(2)}) collective-permute-start(bf16[4032,128]{1,0:T(8,128)(2,1)S(1)} %get-tuple-element.138.refs_0_), channel_id=1, source_target_pairs={{0,1},{1,0},{2,3},{3,2},{4,5},{5,4},{6,7},{7,6},{8,9},{9,8},{10,11... | collective-permute-start | bytes 3096584 | tf_op jit(solution)/shard_map/ppermute | solution.py:860
  152.3 15.0 %collective-permute-start.11 = (bf16[128,960]{1,0:T(8,128)(2,1)S(1)}, bf16[128,960]{1,0:T(8,128)(2,1)S(1)}, u32[]{:S(2)}, u32[]{:S(2)}) collective-permute-start(bf16[128,960]{1,0:T(8,128)(2,1)S(1)} %get-tuple-element.135), channel_id=1, source_target_pairs={{0,1},{1,0},{2,3},{3,2},{4,5},{5,4},{6,7},{7,6},{8,9},{9,8},{10,11... | collective-permute-start | bytes 737288 | tf_op jit(solution)/shard_map/ppermute | solution.py:860
  152.3 15.0 %collective-permute-start.12 = (bf16[128,960]{1,0:T(8,128)(2,1)S(1)}, bf16[128,960]{1,0:T(8,128)(2,1)S(1)}, u32[]{:S(2)}, u32[]{:S(2)}) collective-permute-start(bf16[128,960]{1,0:T(8,128)(2,1)S(1)} %get-tuple-element.136), channel_id=1, source_target_pairs={{0,2},{1,3},{2,0},{3,1},{4,6},{5,7},{6,4},{7,5},{8,10},{9,11},{10,... | collective-permute-start | bytes 737288 | tf_op jit(solution)/shard_map/ppermute | solution.py:860
  155.9 11.4 %collective-permute-start.13 = (bf16[128,960]{1,0:T(8,128)(2,1)S(1)}, bf16[128,960]{1,0:T(8,128)(2,1)S(1)}, u32[]{:S(2)}, u32[]{:S(2)}) collective-permute-start(bf16[128,960]{1,0:T(8,128)(2,1)S(1)} %get-tuple-element.137), channel_id=1, source_target_pairs={{0,3},{1,2},{2,1},{3,0},{4,7},{5,6},{6,5},{7,4},{8,11},{9,10},{10,... | collective-permute-start | bytes 737288 | tf_op jit(solution)/shard_map/ppermute | solution.py:860
  177.0 14.3 %collective-permute-start.17 = (bf16[2,768,384]{2,1,0:T(8,128)(2,1)S(1)}, bf16[2,768,384]{2,1,0:T(8,128)(2,1)S(1)}, u32[]{:S(2)}, u32[]{:S(2)}) collective-permute-start(bf16[2,768,384]{2,1,0:T(8,128)(2,1)S(1)} %get-tuple-element.155), channel_id=1, source_target_pairs={{0,1},{1,0},{2,3},{3,2},{4,5},{5,4},{6,7},{7,6},{8,9},{9,8},{10,11... | collective-permute-start | bytes 3538952 | tf_op jit(solution)/shard_map/ppermute | solution.py:860
  180.1 16.4 %collective-permute-start.18 = (bf16[4,96,768]{2,1,0:T(8,128)(2,1)}, bf16[4,96,768]{2,1,0:T(8,128)(2,1)S(1)}, u32[]{:S(2)}, u32[]{:S(2)}) collective-permute-start(bf16[4,96,768]{2,1,0:T(8,128)(2,1)} %copy-done.18), channel_id=1, source_target_pairs={{0,4},{1,5},{2,6},{3,7},{4,0},{5,1},{6,2},{7,3},{8,12},{9,13},{10,... | collective-permute-start | bytes 1769480 | tf_op jit(solution)/shard_map/ppermute | solution.py:860
  181.8 16.4 %collective-permute-start.19 = (bf16[4,96,768]{2,1,0:T(8,128)(2,1)}, bf16[4,96,768]{2,1,0:T(8,128)(2,1)S(1)}, u32[]{:S(2)}, u32[]{:S(2)}) collective-permute-start(bf16[4,96,768]{2,1,0:T(8,128)(2,1)} %copy-done.17), channel_id=1, source_target_pairs={{0,8},{1,9},{2,10},{3,11},{4,12},{5,13},{6,14},{7,15},{8,0},{9,1},... | collective-permute-start | bytes 1769480 | tf_op jit(solution)/shard_map/ppermute | solution.py:860
  189.1 27.2 %collective-permute-start.23 = (bf16[4,112,576]{2,1,0:T(8,128)(2,1)S(1)}, bf16[4,112,576]{2,1,0:T(8,128)(2,1)S(1)}, u32[]{:S(2)}, u32[]{:S(2)}) collective-permute-start(bf16[4,112,576]{2,1,0:T(8,128)(2,1)S(1)} %get-tuple-element.153), channel_id=1, source_target_pairs={{0,4},{1,5},{2,6},{3,7},{4,0},{5,1},{6,2},{7,3},{8,12},{9,13},{10,... | collective-permute-start | bytes 1548296 | tf_op jit(solution)/shard_map/ppermute | solution.py:860
  190.5 25.8 %collective-permute-start.24 = (bf16[4,112,576]{2,1,0:T(8,128)(2,1)S(1)}, bf16[4,112,576]{2,1,0:T(8,128)(2,1)S(1)}, u32[]{:S(2)}, u32[]{:S(2)}) collective-permute-start(bf16[4,112,576]{2,1,0:T(8,128)(2,1)S(1)} %get-tuple-element.173), channel_id=1, source_target_pairs={{0,8},{1,9},{2,10},{3,11},{4,12},{5,13},{6,14},{7,15},{8,0},{9,1},... | collective-permute-start | bytes 1548296 | tf_op jit(solution)/shard_map/ppermute | solution.py:860
  199.1 16.5 %collective-permute-start.21 = (bf16[2,96,768]{2,1,0:T(8,128)(2,1)S(1)}, bf16[2,96,768]{2,1,0:T(8,128)(2,1)S(1)}, u32[]{:S(2)}, u32[]{:S(2)}) collective-permute-start(bf16[2,96,768]{2,1,0:T(8,128)(2,1)S(1)} %get-tuple-element.160), channel_id=1, source_target_pairs={{0,8},{1,9},{2,10},{3,11},{4,12},{5,13},{6,14},{7,15},{8,0},{9,1},... | collective-permute-start | bytes 884744 | tf_op jit(solution)/shard_map/ppermute | solution.py:860
  199.2 12.9 %collective-permute-start.20 = (bf16[768,384]{1,0:T(8,128)(2,1)S(1)}, bf16[768,384]{1,0:T(8,128)(2,1)S(1)}, u32[]{:S(2)}, u32[]{:S(2)}) collective-permute-start(bf16[768,384]{1,0:T(8,128)(2,1)S(1)} %get-tuple-element.165), channel_id=1, source_target_pairs={{0,2},{1,3},{2,0},{3,1},{4,6},{5,7},{6,4},{7,5},{8,10},{9,11},{10,... | collective-permute-start | bytes 1769480 | tf_op jit(solution)/shard_map/ppermute | solution.py:860
  199.8 15.8 %collective-permute-start.22 = (bf16[2,96,768]{2,1,0:T(8,128)(2,1)S(1)}, bf16[2,96,768]{2,1,0:T(8,128)(2,1)S(1)}, u32[]{:S(2)}, u32[]{:S(2)}) collective-permute-start(bf16[2,96,768]{2,1,0:T(8,128)(2,1)S(1)} %get-tuple-element.169), channel_id=1, source_target_pairs={{0,4},{1,5},{2,6},{3,7},{4,0},{5,1},{6,2},{7,3},{8,12},{9,13},{10,... | collective-permute-start | bytes 884744 | tf_op jit(solution)/shard_map/ppermute | solution.py:860
  217.1 15.4 %collective-permute-start.26 = (bf16[2,112,576]{2,1,0:T(8,128)(2,1)S(1)}, bf16[2,112,576]{2,1,0:T(8,128)(2,1)S(1)}, u32[]{:S(2)}, u32[]{:S(2)}) collective-permute-start(bf16[2,112,576]{2,1,0:T(8,128)(2,1)S(1)} %get-tuple-element.176), channel_id=1, source_target_pairs={{0,8},{1,9},{2,10},{3,11},{4,12},{5,13},{6,14},{7,15},{8,0},{9,1},... | collective-permute-start | bytes 774152 | tf_op jit(solution)/shard_map/ppermute | solution.py:860
  217.9 14.6 %collective-permute-start.27 = (bf16[2,112,576]{2,1,0:T(8,128)(2,1)S(1)}, bf16[2,112,576]{2,1,0:T(8,128)(2,1)S(1)}, u32[]{:S(2)}, u32[]{:S(2)}) collective-permute-start(bf16[2,112,576]{2,1,0:T(8,128)(2,1)S(1)} %get-tuple-element.181), channel_id=1, source_target_pairs={{0,4},{1,5},{2,6},{3,7},{4,0},{5,1},{6,2},{7,3},{8,12},{9,13},{10,... | collective-permute-start | bytes 774152 | tf_op jit(solution)/shard_map/ppermute | solution.py:860
  218.7 16.8 %collective-permute-start.29 = (bf16[2,96,768]{2,1,0:T(8,128)(2,1)S(1)}, bf16[2,96,768]{2,1,0:T(8,128)(2,1)S(1)}, u32[]{:S(2)}, u32[]{:S(2)}) collective-permute-start(bf16[2,96,768]{2,1,0:T(8,128)(2,1)S(1)} %get-tuple-element.170), channel_id=1, source_target_pairs={{0,16},{1,17},{2,18},{3,19},{4,20},{5,21},{6,22},{7,23},{8,24},{9,... | collective-permute-start | bytes 884744 | tf_op jit(solution)/shard_map/ppermute | solution.py:860
  222.6 12.1 %collective-permute-start.28 = (bf16[2,96,384]{2,1,0:T(8,128)(2,1)S(1)}, bf16[2,96,384]{2,1,0:T(8,128)(2,1)S(1)}, u32[]{:S(2)}, u32[]{:S(2)}) collective-permute-start(bf16[2,96,384]{2,1,0:T(8,128)(2,1)S(1)} %get-tuple-element.178), channel_id=1, source_target_pairs={{0,8},{1,9},{2,10},{3,11},{4,12},{5,13},{6,14},{7,15},{8,0},{9,1},... | collective-permute-start | bytes 442376 | tf_op jit(solution)/shard_map/ppermute | solution.py:860
  233.2 15.2 %collective-permute-start.30 = (bf16[2,112,576]{2,1,0:T(8,128)(2,1)S(1)}, bf16[2,112,576]{2,1,0:T(8,128)(2,1)S(1)}, u32[]{:S(2)}, u32[]{:S(2)}) collective-permute-start(bf16[2,112,576]{2,1,0:T(8,128)(2,1)S(1)} %get-tuple-element.185), channel_id=1, source_target_pairs={{0,16},{1,17},{2,18},{3,19},{4,20},{5,21},{6,22},{7,23},{8,24},{9,... | collective-permute-start | bytes 774152 | tf_op jit(solution)/shard_map/ppermute | solution.py:860
  235.5 13.1 %collective-permute-start.33 = (bf16[2,96,768]{2,1,0:T(8,128)(2,1)S(1)}, bf16[2,96,768]{2,1,0:T(8,128)(2,1)S(1)}, u32[]{:S(2)}, u32[]{:S(2)}) collective-permute-start(bf16[2,96,768]{2,1,0:T(8,128)(2,1)S(1)} %shard_map.342.refs_0_), channel_id=1, source_target_pairs={{0,2},{1,3},{2,0},{3,1},{4,6},{5,7},{6,4},{7,5},{8,10},{9,11},{10,... | collective-permute-start | bytes 884744 | tf_op jit(solution)/shard_map/ppermute | solution.py:860
  236.2 13.0 %collective-permute-start.31 = (bf16[1,96,384]{2,1,0:T(8,128)(2,1)S(1)}, bf16[1,96,384]{2,1,0:T(8,128)(2,1)S(1)}, u32[]{:S(2)}, u32[]{:S(2)}) collective-permute-start(bf16[1,96,384]{2,1,0:T(8,128)(2,1)S(1)} %get-tuple-element.187), channel_id=1, source_target_pairs={{0,16},{1,17},{2,18},{3,19},{4,20},{5,21},{6,22},{7,23},{8,24},{9,... | collective-permute-start | bytes 221192 | tf_op jit(solution)/shard_map/ppermute | solution.py:860
  (62 other events, 320.7 us)
where the time goes:
time: 267 us; the launch traced here: 262 us
  Pallas kernels  74.3 us (28%)
  waiting for transfers between devices  63.6 us (24%)
  starting transfers between devices  46.5 us (17%)
  local copies, waits for them, and re-layouts  38.4 us (14%)
  blocking collectives  36.6 us (14%)
    pallas_call x26, Pallas kernels, local_kernel(): pl.pallas_call(body, out_shape=list(out_shape), in_specs=[pl.BlockSpec(me...  74.3 us
    ppermute x41, waiting for transfers between devices, hop(): return lax.ppermute(array, AXES, pairs)  63.6 us
    ppermute x41, starting transfers between devices, hop(): return lax.ppermute(array, AXES, pairs)  39 us
    unnamed x1, blocking collectives  36.6 us
    unnamed x107, local copies, waits for them, and re-layouts  33 us
    all_to_all x1, starting transfers between devices, fast_on_device(): lax.all_to_all(parcels_out, 'stream', split_axis=0, concat_axis=0, tiled=...  7.41 us
  transfers between devices with their start and end apart: 42, of which 15 were waited for; matrix products, arithmetic and copies ran while one was open for 3% of the time, Pallas kernels for 22%

commit v1 on v0

--- a/solution.py
+++ b/solution.py
@@ -814,11 +814,11 @@
                 out[q * tall : (q + 1) * tall, :] = part
 
 
-ORDER = ('dq', 'self', 'owner', 'ff1', 'kv0', 'rest1', 'kv1', 'ff2', 'memory', 'kv2', 'ff3', 'rest2', 'kv3', 'rest3', 'kv4', 'ff4', 'rest4', 'kv5', 'lay_ff', 'lay_rest', 'lay_kv')
+ORDER = ('dq', 'self', 'owner', 'ff1', 'kv0', 'rest1', 'kv1', 'ff2', 'kv2', 'ff3', 'rest2', 'kv3', 'memory', 'rest3', 'kv4', 'ff4', 'rest4', 'kv5', 'lay_ff', 'lay_rest', 'lay_kv')
 BEFORE = {'cross': ('early',), 'ffn': ('qc_z',), 'self': ('qc_y', 'do_stack'), 'ff1': ('exports',)}
 RELAY = ()
 COSTS = {'deal': 2, 'self_forward': 5, 'own_keys': 6, 'cross': 17, 'ffn': 12, 'dq': 20, 'self': 12, 'ff1': 5, 'rest1': 5, 'owner': 12, 'kv0': 7, 'memory': 6}
-LIMITS = {}
+LIMITS = {'self': 46}
 
 
 def fast_on_device(

time: 267 us -> 265 us (level)
    unnamed x107 -> x105, local copies, waits for them, and re-layouts: 33 us -> 31.4 us
  transfers between devices with their start and end apart: 42 -> 42, of which waited for: 15 -> 14; matrix products, arithmetic and copies ran while one was open for 3% -> 3% of each run, Pallas kernels for 22% -> 23%
where the time goes in v1:
time: 265 us; the launch traced here: 260 us
  Pallas kernels  76.4 us (29%)
  waiting for transfers between devices  63.4 us (24%)
  starting transfers between devices  44 us (17%)
  local copies, waits for them, and re-layouts  36.7 us (14%)
  blocking collectives  36.6 us (14%)
    pallas_call x26, Pallas kernels, local_kernel(): pl.pallas_call(body, out_shape=list(out_shape), in_specs=[pl.BlockSpec(me...  76.4 us
    ppermute x41, waiting for transfers between devices, hop(): return lax.ppermute(array, AXES, pairs)  63.4 us
    ppermute x41, starting transfers between devices, hop(): return lax.ppermute(array, AXES, pairs)  36.6 us
    unnamed x1, blocking collectives  36.6 us
    unnamed x105, local copies, waits for them, and re-layouts  31.4 us
    all_to_all x1, starting transfers between devices, fast_on_device(): lax.all_to_all(parcels_out, 'stream', split_axis=0, concat_axis=0, tiled=...  7.41 us
  transfers between devices with their start and end apart: 42, of which 14 were waited for; matrix products, arithmetic and copies ran while one was open for 3% of the time, Pallas kernels for 23%

profile of v1, /device:TPU:0, one launch (start us, length us, event | category | flops | bytes accessed | tf_op | source)
XLA Modules:
  0.0 260.3 jit_solution(15107552017294760927)
XLA Ops:
  5.2 7.4 %all-to-all-start = ((bf16[8,256,768]{2,1,0:T(8,128)(2,1)}), bf16[8,256,768]{2,1,0:T(8,128)(2,1)S(1)}, u32[]{:S(2)}, u32[]{:S(2)}) async-start(bf16[8,256,768]{2,1,0:T(8,128)(2,1)} %copy-done), calls=%async_computation | async-start | bytes 6291456 | tf_op jit(solution)/shard_map/all_to_all | solution.py:883
  12.7 2.0 copy-done.3
  17.2 3.0 %shard_map.323 = (bf16[128,2304]{1,0:T(8,128)(2,1)S(1)}, f32[128,768]{1,0:T(8,128)S(1)}, bf16[128,768]{1,0:T(8,128)(2,1)S(1)}, bf16[128,768]{1,0:T(8,128)(2,1)S(1)}, bf16[2304,128]{1,0:T(8,128)(2,1)}) custom-call(bf16[128,768]{1,0:T(8,128)(2,1)S(1)} %bitcast.47, bf16[768,2304]{1,0:T(8,128)(2,1)S(1)} %copy-done.3, bf16[768,768]{1,0:T(8,128)(2,1)S(1)} %copy-done.10, ...), custom_call_target="tpu_custom_call" | custom-call | flops 5750000128 | bytes 500000 | tf_op jit(solution)/shard_map/pallas_call | solution.py:338
  29.4 8.2 %collective-permute-done.1.refs_2_ = bf16[2304,128]{1,0:T(8,128)(2,1)} collective-permute-done((bf16[2304,128]{1,0:T(8,128)(2,1)}, bf16[2304,128]{1,0:T(8,128)(2,1)}, u32[]{:S(2)}, u32[]{:S(2)}) %collective-permute-start.1) | collective-permute-done | bytes 589856 | tf_op jit(solution)/shard_map/ppermute | solution.py:860
  40.7 2.6 %shard_map.324 = (bf16[1024,1536]{1,0:T(8,128)(2,1)S(1)}, bf16[768,1024]{1,0:T(8,128)(2,1)S(1)}) custom-call(bf16[1024,768]{1,0:T(8,128)(2,1)S(1)} %bitcast.46, bf16[768,1536]{1,0:T(8,128)(2,1)S(1)} %copy-done.4), custom_call_target="tpu_custom_call" | custom-call | flops 6899999744 | bytes 600000 | tf_op jit(solution)/shard_map/pallas_call | solution.py:338
  47.1 36.6 %all-reduce.1 = s32[64]{0:T(128)S(1)} all-reduce(s32[64]{0:T(128)S(1)} %dynamic-update-slice), channel_id=2, replica_groups=mesh['stream'=8,'rep'=4] {'stream'}, use_global_device_ids=true, to_apply=%add.1 | all-reduce | flops 64 | bytes 512
  83.8 2.8 %collective-permute-start.4 = (bf16[128,768]{1,0:T(8,128)(2,1)S(1)}, bf16[128,768]{1,0:T(8,128)(2,1)S(1)}, u32[]{:S(2)}, u32[]{:S(2)}) collective-permute-start(bf16[128,768]{1,0:T(8,128)(2,1)S(1)} %get-tuple-element.124.qc), channel_id=1, source_target_pairs={{0,16},{1,17},{2,18},{3,19},{4,20},{5,21},{6,22},{7,23},{8,24},{9,... | collective-permute-start | bytes 589832 | tf_op jit(solution)/shard_map/ppermute | solution.py:860
  89.8 11.1 %shard_map.325 = (bf16[128,768]{1,0:T(8,128)(2,1)S(1)}, bf16[2048,1536]{1,0:T(8,128)(2,1)S(1)}, f32[256,128]{1,0:T(8,128)S(1)}, f32[8,2048]{1,0:T(8,128)S(1)}) custom-call(s32[8,8]{1,0:T(8,128)S(1)} %reshape.89.routes_ref, s32[1]{0:T(128)} %bitcast.5.me_ref, bf16[128,768]{1,0:T(8,128)(2,1)S(1)} %get-tuple-element.124.qc, ...), custom_call_target="tpu_custom_call" | custom-call | flops 19549999104 | bytes 1700000 | tf_op jit(solution)/shard_map/pallas_call | solution.py:338
  101.1 2.3 copy-done.1
  103.4 2.3 copy-done.2
  105.7 7.5 %shard_map.326 = (bf16[128,768]{1,0:T(8,128)(2,1)}, f32[128,768]{1,0:T(8,128)S(1)}, bf16[144,768]{1,0:T(8,128)(2,1)S(1)}, f32[256,128]{1,0:T(8,128)S(1)}, f32[8,...) custom-call(s32[1]{0:T(128)} %bitcast.rep_ref, ...), custom_call_target="tpu_custom_call" | custom-call | flops 13799999488 | bytes 1200000 | tf_op jit(solution)/shard_map/pallas_call | solution.py:338
  113.2 2.3 collective-permute-start.9
  115.5 2.8 %collective-permute-start.8 = (bf16[144,768]{1,0:T(8,128)(2,1)S(1)}, bf16[144,768]{1,0:T(8,128)(2,1)S(1)}, u32[]{:S(2)}, u32[]{:S(2)}) collective-permute-start(bf16[144,768]{1,0:T(8,128)(2,1)S(1)} %get-tuple-element.125.do2), channel_id=1, source_target_pairs={{0,16},{1,17},{2,18},{3,19},{4,20},{5,21},{6,22},{7,23},{8,24},{9,... | collective-permute-start | bytes 663560 | tf_op jit(solution)/shard_map/ppermute | solution.py:860
  120.8 8.9 %shard_map.327.dqc_ref = bf16[128,768]{1,0:T(8,128)(2,1)S(1)} custom-call(bf16[128,768]{1,0:T(8,128)(2,1)S(1)} %get-tuple-element.124.qc, bf16[144,768]{1,0:T(8,128)(2,1)S(1)} %get-tuple-element.125.do2, bf16[2048,1536]{1,0:T(8,128)(2,1)S(1)} %get-tuple-element.126.kv, f32[8,2048]{1,0:T(8,128)S(1)} %get-tuple-element.127.bias_ref, ...), custom_call_target="tpu_custom_call" | custom-call | flops 23000000512 | bytes 2000000 | tf_op jit(solution)/shard_map/pallas_call | solution.py:338
  129.7 4.9 %collective-permute-done.8 = bf16[144,768]{1,0:T(8,128)(2,1)S(1)} collective-permute-done((bf16[144,768]{1,0:T(8,128)(2,1)S(1)}, bf16[144,768]{1,0:T(8,128)(2,1)S(1)}, u32[]{:S(2)}, u32[]{:S(2)}) %collective-permute-start.8) | collective-permute-done | bytes 221216 | tf_op jit(solution)/shard_map/ppermute | solution.py:860
  136.7 8.6 %shard_map.328 = (f32[128,768]{1,0:T(8,128)}, f32[8,768]{1,0:T(8,128)S(1)}, bf16[128,960]{1,0:T(8,128)(2,1)S(1)}, bf16[128,960]{1,0:T(8,128)(2,1)S(1)}, bf16[128...) custom-call(s32[1]{0:T(128)} %bitcast.rep_ref, bf16[128,768]{1,0:T(8,128)(2,1)S(1)} %shard_map.327.dqc_ref, ...), custom_call_target="tpu_custom_call" | custom-call | flops 13799999488 | bytes 1200000 | tf_op jit(solution)/shard_map/pallas_call | solution.py:338
  146.0 5.7 %collective-permute-done.15.refs_2_ = bf16[5760,128]{1,0:T(8,128)(2,1)S(1)} collective-permute-done((bf16[5760,128]{1,0:T(8,128)(2,1)S(1)}, bf16[5760,128]{1,0:T(8,128)(2,1)S(1)}, u32[]{:S(2)}, u32[]{:S(2)}) %collective-permute-start.15) | collective-permute-done | bytes 1474592 | tf_op jit(solution)/shard_map/ppermute | solution.py:860
  153.8 2.1 collective-permute-done.10.refs_3_
  155.9 11.4 %shard_map.329.dkv = bf16[1024,1536]{1,0:T(8,128)(2,1)S(1)} custom-call(s32[8]{0:T(128)S(1)} %broadcast_xor_fusion.where_ref, bf16[4,128,768]{2,1,0:T(8,128)(2,1)S(1)} %pad_maximum_fusion.1.refs_0_, bf16[4,128,768]{2,1,0:T(8,128)(2,1)S(1)} %collective-permute-done.6.refs_1_, bf16[4,144,768]{2,1,0:T(8,128)(2,1)S(1)} %pad_maximum_fusion.refs_2_, ...), custom_call_target="tpu_custom_call" | custom-call | flops 13799999488 | bytes 1200000 | tf_op jit(solution)/shard_map/pallas_call | solution.py:338
  167.4 2.6 %shard_map.330 = (bf16[4,96,768]{2,1,0:T(8,128)(2,1)S(1)}, bf16[4,96,768]{2,1,0:T(8,128)(2,1)S(1)}, bf16[4,96,768]{2,1,0:T(8,128)(2,1)S(1)}, bf16[4,96,768]{2,1,0:T(8,128)(2,1)S(1)}, bf16[768,192]{1,0:T(8,128)(2,1)S(1)}) custom-call(s32[3]{0:T(128)S(1)} %pad_add_fusion.bits_ref, bf16[4032,128]{1,0:T(8,128)(2,1)S(1)} %get-tuple-element.138.refs_0_, ...), custom_call_target="tpu_custom_call" | custom-call | flops 5750000128 | bytes 500000 | tf_op jit(solution)/shard_map/pallas_call | solution.py:338
  170.1 3.4 %shard_map.331 = (bf16[2,768,384]{2,1,0:T(8,128)(2,1)S(1)}, bf16[2,768,384]{2,1,0:T(8,128)(2,1)S(1)}) custom-call(s32[1]{0:T(128)} %bitcast.rep_ref, bf16[1024,1536]{1,0:T(8,128)(2,1)S(1)} %shard_map.329.dkv, bf16[768,1024]{1,0:T(8,128)(2,1)S(1)} %copy-done.37), custom_call_target="tpu_custom_call" | custom-call | flops 8049999872 | bytes 700000 | tf_op jit(solution)/shard_map/pallas_call | solution.py:338
  183.3 3.3 %shard_map.332 = (bf16[4,112,576]{2,1,0:T(8,128)(2,1)S(1)}, bf16[4,112,576]{2,1,0:T(8,128)(2,1)S(1)}, bf16[4,112,576]{2,1,0:T(8,128)(2,1)S(1)}, bf16[4,112,576]{2,1,0:T(8,128)(2,1)S(1)}) custom-call(s32[3]{0:T(128)S(1)} %pad_add_fusion.bits_ref, bf16[2304,128]{1,0:T(8,128)(2,1)} %get-tuple-element.147.refs_0_, ...), custom_call_target="tpu_custom_call" | custom-call | flops 5750000128 | bytes 500000 | tf_op jit(solution)/shard_map/pallas_call | solution.py:338
  189.8 4.3 %collective-permute-done.18.got0 = bf16[4,96,768]{2,1,0:T(8,128)(2,1)S(1)} collective-permute-done((bf16[4,96,768]{2,1,0:T(8,128)(2,1)}, bf16[4,96,768]{2,1,0:T(8,128)(2,1)S(1)}, u32[]{:S(2)}, u32[]{:S(2)}) %collective-permute-start.18) | collective-permute-done | bytes 589856 | tf_op jit(solution)/shard_map/ppermute | solution.py:860
  194.1 1.8 collective-permute-done.19.got1
  198.2 3.7 %collective-permute-done.20.got = bf16[768,384]{1,0:T(8,128)(2,1)S(1)} collective-permute-done((bf16[768,384]{1,0:T(8,128)(2,1)S(1)}, bf16[768,384]{1,0:T(8,128)(2,1)S(1)}, u32[]{:S(2)}, u32[]{:S(2)}) %collective-permute-start.20) | collective-permute-done | bytes 589856 | tf_op jit(solution)/shard_map/ppermute | solution.py:860
  203.9 9.4 %collective-permute-done.21.refs_1_ = bf16[2,96,768]{2,1,0:T(8,128)(2,1)S(1)} collective-permute-done((bf16[2,96,768]{2,1,0:T(8,128)(2,1)S(1)}, bf16[2,96,768]{2,1,0:T(8,128)(2,1)S(1)}, u32[]{:S(2)}, u32[]{:S(2)}) %collective-permute-start.21) | collective-permute-done | bytes 294944 | tf_op jit(solution)/shard_map/ppermute | solution.py:860
  213.9 1.9 collective-permute-start.29
  216.6 2.2 collective-permute-start.26
  221.4 3.8 %shard_map.339 = bf16[1024,768]{1,0:T(8,128)(2,1)} custom-call(bf16[1024,1536]{1,0:T(8,128)(2,1)S(1)} %copy-done.33, bf16[768,1536]{1,0:T(8,128)(2,1)S(1)} %copy-done.6), custom_call_target="tpu_custom_call" | custom-call | flops 6899999744 | bytes 600000 | tf_op jit(solution)/shard_map/pallas_call | solution.py:338
  225.2 9.0 %collective-permute-done.26.refs_1_ = bf16[2,112,576]{2,1,0:T(8,128)(2,1)S(1)} collective-permute-done((bf16[2,112,576]{2,1,0:T(8,128)(2,1)S(1)}, bf16[2,112,576]{2,1,0:T(8,128)(2,1)S(1)}, u32[]{:S(2)}, u32[]{:S(2)}) %collective-permute-start.26) | collective-permute-done | bytes 258080 | tf_op jit(solution)/shard_map/ppermute | solution.py:860
  239.2 7.0 %collective-permute-done.30.got = bf16[2,112,576]{2,1,0:T(8,128)(2,1)S(1)} collective-permute-done((bf16[2,112,576]{2,1,0:T(8,128)(2,1)S(1)}, bf16[2,112,576]{2,1,0:T(8,128)(2,1)S(1)}, u32[]{:S(2)}, u32[]{:S(2)}) %collective-permute-start.30) | collective-permute-done | bytes 258080 | tf_op jit(solution)/shard_map/ppermute | solution.py:860
  249.0 4.8 %collective-permute-done.36.refs_2_ = bf16[2,112,576]{2,1,0:T(8,128)(2,1)S(1)} collective-permute-done((bf16[2,112,576]{2,1,0:T(8,128)(2,1)S(1)}, bf16[2,112,576]{2,1,0:T(8,128)(2,1)S(1)}, u32[]{:S(2)}, u32[]{:S(2)}) %collective-permute-start.36) | collective-permute-done | bytes 258080 | tf_op jit(solution)/shard_map/ppermute | solution.py:860
  (210 shorter events, 68.2 us)
Async XLA Ops:
  5.2 78.5 %all-to-all-start = ((bf16[8,256,768]{2,1,0:T(8,128)(2,1)}), bf16[8,256,768]{2,1,0:T(8,128)(2,1)S(1)}, u32[]{:S(2)}, u32[]{:S(2)}) async-start(bf16[8,256,768]{2,1,0:T(8,128)(2,1)} %copy-done), calls=%async_computation | async-start | bytes 6291456 | tf_op jit(solution)/shard_map/all_to_all | solution.py:883
  22.5 15.1 %collective-permute-start.1 = (bf16[2304,128]{1,0:T(8,128)(2,1)}, bf16[2304,128]{1,0:T(8,128)(2,1)}, u32[]{:S(2)}, u32[]{:S(2)}) collective-permute-start(bf16[2304,128]{1,0:T(8,128)(2,1)} %get-tuple-element.147.refs_0_), channel_id=1, source_target_pairs={{0,2},{1,3},{2,0},{3,1},{4,6},{5,7},{6,4},{7,5},{8,10},{9,11},{10,... | collective-permute-start | bytes 1769480 | tf_op jit(solution)/shard_map/ppermute | solution.py:860
  24.0 22.1 %collective-permute-start = (bf16[2304,128]{1,0:T(8,128)(2,1)}, bf16[2304,128]{1,0:T(8,128)(2,1)}, u32[]{:S(2)}, u32[]{:S(2)}) collective-permute-start(bf16[2304,128]{1,0:T(8,128)(2,1)} %get-tuple-element.147.refs_0_), channel_id=1, source_target_pairs={{0,1},{1,0},{2,3},{3,2},{4,5},{5,4},{6,7},{7,6},{8,9},{9,8},{10,11... | collective-permute-start | bytes 1769480 | tf_op jit(solution)/shard_map/ppermute | solution.py:860
  83.8 17.2 %collective-permute-start.3 = (bf16[128,768]{1,0:T(8,128)(2,1)S(1)}, bf16[128,768]{1,0:T(8,128)(2,1)S(1)}, u32[]{:S(2)}, u32[]{:S(2)}) collective-permute-start(bf16[128,768]{1,0:T(8,128)(2,1)S(1)} %get-tuple-element.124.qc), channel_id=1, source_target_pairs={{0,8},{1,9},{2,10},{3,11},{4,12},{5,13},{6,14},{7,15},{8,0},{9,1},... | collective-permute-start | bytes 589832 | tf_op jit(solution)/shard_map/ppermute | solution.py:860
  83.8 17.2 %collective-permute-start.4 = (bf16[128,768]{1,0:T(8,128)(2,1)S(1)}, bf16[128,768]{1,0:T(8,128)(2,1)S(1)}, u32[]{:S(2)}, u32[]{:S(2)}) collective-permute-start(bf16[128,768]{1,0:T(8,128)(2,1)S(1)} %get-tuple-element.124.qc), channel_id=1, source_target_pairs={{0,16},{1,17},{2,18},{3,19},{4,20},{5,21},{6,22},{7,23},{8,24},{9,... | collective-permute-start | bytes 589832 | tf_op jit(solution)/shard_map/ppermute | solution.py:860
  86.6 14.4 %collective-permute-start.5 = (bf16[128,768]{1,0:T(8,128)(2,1)S(1)}, bf16[128,768]{1,0:T(8,128)(2,1)S(1)}, u32[]{:S(2)}, u32[]{:S(2)}) collective-permute-start(bf16[128,768]{1,0:T(8,128)(2,1)S(1)} %get-tuple-element.124.qc), channel_id=1, source_target_pairs={{0,24},{1,25},{2,26},{3,27},{4,28},{5,29},{6,30},{7,31},{8,16},{9,... | collective-permute-start | bytes 589832 | tf_op jit(solution)/shard_map/ppermute | solution.py:860
  113.2 16.5 %collective-permute-start.9 = (bf16[144,768]{1,0:T(8,128)(2,1)S(1)}, bf16[144,768]{1,0:T(8,128)(2,1)S(1)}, u32[]{:S(2)}, u32[]{:S(2)}) collective-permute-start(bf16[144,768]{1,0:T(8,128)(2,1)S(1)} %get-tuple-element.125.do2), channel_id=1, source_target_pairs={{0,24},{1,25},{2,26},{3,27},{4,28},{5,29},{6,30},{7,31},{8,16},{9,... | collective-permute-start | bytes 663560 | tf_op jit(solution)/shard_map/ppermute | solution.py:860
  115.5 19.1 %collective-permute-start.8 = (bf16[144,768]{1,0:T(8,128)(2,1)S(1)}, bf16[144,768]{1,0:T(8,128)(2,1)S(1)}, u32[]{:S(2)}, u32[]{:S(2)}) collective-permute-start(bf16[144,768]{1,0:T(8,128)(2,1)S(1)} %get-tuple-element.125.do2), channel_id=1, source_target_pairs={{0,16},{1,17},{2,18},{3,19},{4,20},{5,21},{6,22},{7,23},{8,24},{9,... | collective-permute-start | bytes 663560 | tf_op jit(solution)/shard_map/ppermute | solution.py:860
  118.3 16.3 %collective-permute-start.7 = (bf16[144,768]{1,0:T(8,128)(2,1)S(1)}, bf16[144,768]{1,0:T(8,128)(2,1)S(1)}, u32[]{:S(2)}, u32[]{:S(2)}) collective-permute-start(bf16[144,768]{1,0:T(8,128)(2,1)S(1)} %get-tuple-element.125.do2), channel_id=1, source_target_pairs={{0,8},{1,9},{2,10},{3,11},{4,12},{5,13},{6,14},{7,15},{8,0},{9,1},... | collective-permute-start | bytes 663560 | tf_op jit(solution)/shard_map/ppermute | solution.py:860
  118.5 18.1 %collective-permute-start.6 = (bf16[4,128,768]{2,1,0:T(8,128)(2,1)S(1)}, bf16[4,128,768]{2,1,0:T(8,128)(2,1)S(1)}, u32[]{:S(2)}, u32[]{:S(2)}) collective-permute-start(bf16[4,128,768]{2,1,0:T(8,128)(2,1)S(1)} %pad_maximum_fusion.1.refs_0_), channel_id=1, source_target_pairs={{0,4},{1,5},{2,6},{3,7},{4,0},{5,1},{6,2},{7,3},{8,12},{9,13},{10,... | collective-permute-start | bytes 2359304 | tf_op jit(solution)/shard_map/ppermute | solution.py:860
  119.3 32.5 %collective-permute-start.15 = (bf16[5760,128]{1,0:T(8,128)(2,1)S(1)}, bf16[5760,128]{1,0:T(8,128)(2,1)S(1)}, u32[]{:S(2)}, u32[]{:S(2)}) collective-permute-start(bf16[5760,128]{1,0:T(8,128)(2,1)S(1)} %get-tuple-element.139), channel_id=1, source_target_pairs={{0,2},{1,3},{2,0},{3,1},{4,6},{5,7},{6,4},{7,5},{8,10},{9,11},{10,... | collective-permute-start | bytes 4423688 | tf_op jit(solution)/shard_map/ppermute | solution.py:860
  134.8 21.1 %collective-permute-start.10 = (bf16[4,144,768]{2,1,0:T(8,128)(2,1)S(1)}, bf16[4,144,768]{2,1,0:T(8,128)(2,1)S(1)}, u32[]{:S(2)}, u32[]{:S(2)}) collective-permute-start(bf16[4,144,768]{2,1,0:T(8,128)(2,1)S(1)} %pad_maximum_fusion.refs_2_), channel_id=1, source_target_pairs={{0,4},{1,5},{2,6},{3,7},{4,0},{5,1},{6,2},{7,3},{8,12},{9,13},{10,... | collective-permute-start | bytes 2654216 | tf_op jit(solution)/shard_map/ppermute | solution.py:860
  151.7 15.6 %collective-permute-start.16 = (bf16[5760,128]{1,0:T(8,128)(2,1)S(1)}, bf16[5760,128]{1,0:T(8,128)(2,1)S(1)}, u32[]{:S(2)}, u32[]{:S(2)}) collective-permute-start(bf16[5760,128]{1,0:T(8,128)(2,1)S(1)} %collective-permute-done.15.refs_2_), channel_id=1, source_target_pairs={{0,1},{1,0},{2,3},{3,2},{4,5},{5,4},{6,7},{7,6},{8,9},{9,8},{10,11... | collective-permute-start | bytes 4423688 | tf_op jit(solution)/shard_map/ppermute | solution.py:860
  151.8 15.6 %collective-permute-start.14 = (bf16[4032,128]{1,0:T(8,128)(2,1)S(1)}, bf16[4032,128]{1,0:T(8,128)(2,1)S(1)}, u32[]{:S(2)}, u32[]{:S(2)}) collective-permute-start(bf16[4032,128]{1,0:T(8,128)(2,1)S(1)} %get-tuple-element.138.refs_0_), channel_id=1, source_target_pairs={{0,1},{1,0},{2,3},{3,2},{4,5},{5,4},{6,7},{7,6},{8,9},{9,8},{10,11... | collective-permute-start | bytes 3096584 | tf_op jit(solution)/shard_map/ppermute | solution.py:860
  152.3 15.0 %collective-permute-start.11 = (bf16[128,960]{1,0:T(8,128)(2,1)S(1)}, bf16[128,960]{1,0:T(8,128)(2,1)S(1)}, u32[]{:S(2)}, u32[]{:S(2)}) collective-permute-start(bf16[128,960]{1,0:T(8,128)(2,1)S(1)} %get-tuple-element.135), channel_id=1, source_target_pairs={{0,1},{1,0},{2,3},{3,2},{4,5},{5,4},{6,7},{7,6},{8,9},{9,8},{10,11... | collective-permute-start | bytes 737288 | tf_op jit(solution)/shard_map/ppermute | solution.py:860
  152.3 15.0 %collective-permute-start.12 = (bf16[128,960]{1,0:T(8,128)(2,1)S(1)}, bf16[128,960]{1,0:T(8,128)(2,1)S(1)}, u32[]{:S(2)}, u32[]{:S(2)}) collective-permute-start(bf16[128,960]{1,0:T(8,128)(2,1)S(1)} %get-tuple-element.136), channel_id=1, source_target_pairs={{0,2},{1,3},{2,0},{3,1},{4,6},{5,7},{6,4},{7,5},{8,10},{9,11},{10,... | collective-permute-start | bytes 737288 | tf_op jit(solution)/shard_map/ppermute | solution.py:860
  155.9 11.4 %collective-permute-start.13 = (bf16[128,960]{1,0:T(8,128)(2,1)S(1)}, bf16[128,960]{1,0:T(8,128)(2,1)S(1)}, u32[]{:S(2)}, u32[]{:S(2)}) collective-permute-start(bf16[128,960]{1,0:T(8,128)(2,1)S(1)} %get-tuple-element.137), channel_id=1, source_target_pairs={{0,3},{1,2},{2,1},{3,0},{4,7},{5,6},{6,5},{7,4},{8,11},{9,10},{10,... | collective-permute-start | bytes 737288 | tf_op jit(solution)/shard_map/ppermute | solution.py:860
  174.6 12.1 %collective-permute-start.17 = (bf16[2,768,384]{2,1,0:T(8,128)(2,1)S(1)}, bf16[2,768,384]{2,1,0:T(8,128)(2,1)S(1)}, u32[]{:S(2)}, u32[]{:S(2)}) collective-permute-start(bf16[2,768,384]{2,1,0:T(8,128)(2,1)S(1)} %get-tuple-element.154), channel_id=1, source_target_pairs={{0,1},{1,0},{2,3},{3,2},{4,5},{5,4},{6,7},{7,6},{8,9},{9,8},{10,11... | collective-permute-start | bytes 3538952 | tf_op jit(solution)/shard_map/ppermute | solution.py:860
  177.7 16.4 %collective-permute-start.18 = (bf16[4,96,768]{2,1,0:T(8,128)(2,1)}, bf16[4,96,768]{2,1,0:T(8,128)(2,1)S(1)}, u32[]{:S(2)}, u32[]{:S(2)}) collective-permute-start(bf16[4,96,768]{2,1,0:T(8,128)(2,1)} %copy-done.17), channel_id=1, source_target_pairs={{0,4},{1,5},{2,6},{3,7},{4,0},{5,1},{6,2},{7,3},{8,12},{9,13},{10,... | collective-permute-start | bytes 1769480 | tf_op jit(solution)/shard_map/ppermute | solution.py:860
  179.4 16.4 %collective-permute-start.19 = (bf16[4,96,768]{2,1,0:T(8,128)(2,1)}, bf16[4,96,768]{2,1,0:T(8,128)(2,1)S(1)}, u32[]{:S(2)}, u32[]{:S(2)}) collective-permute-start(bf16[4,96,768]{2,1,0:T(8,128)(2,1)} %copy-done.16), channel_id=1, source_target_pairs={{0,8},{1,9},{2,10},{3,11},{4,12},{5,13},{6,14},{7,15},{8,0},{9,1},... | collective-permute-start | bytes 1769480 | tf_op jit(solution)/shard_map/ppermute | solution.py:860
  187.0 15.0 %collective-permute-start.20 = (bf16[768,384]{1,0:T(8,128)(2,1)S(1)}, bf16[768,384]{1,0:T(8,128)(2,1)S(1)}, u32[]{:S(2)}, u32[]{:S(2)}) collective-permute-start(bf16[768,384]{1,0:T(8,128)(2,1)S(1)} %get-tuple-element.162), channel_id=1, source_target_pairs={{0,2},{1,3},{2,0},{3,1},{4,6},{5,7},{6,4},{7,5},{8,10},{9,11},{10,... | collective-permute-start | bytes 1769480 | tf_op jit(solution)/shard_map/ppermute | solution.py:860
  187.6 28.2 %collective-permute-start.23 = (bf16[4,112,576]{2,1,0:T(8,128)(2,1)S(1)}, bf16[4,112,576]{2,1,0:T(8,128)(2,1)S(1)}, u32[]{:S(2)}, u32[]{:S(2)}) collective-permute-start(bf16[4,112,576]{2,1,0:T(8,128)(2,1)S(1)} %get-tuple-element.152), channel_id=1, source_target_pairs={{0,4},{1,5},{2,6},{3,7},{4,0},{5,1},{6,2},{7,3},{8,12},{9,13},{10,... | collective-permute-start | bytes 1548296 | tf_op jit(solution)/shard_map/ppermute | solution.py:860
  189.0 26.8 %collective-permute-start.24 = (bf16[4,112,576]{2,1,0:T(8,128)(2,1)S(1)}, bf16[4,112,576]{2,1,0:T(8,128)(2,1)S(1)}, u32[]{:S(2)}, u32[]{:S(2)}) collective-permute-start(bf16[4,112,576]{2,1,0:T(8,128)(2,1)S(1)} %get-tuple-element.173), channel_id=1, source_target_pairs={{0,8},{1,9},{2,10},{3,11},{4,12},{5,13},{6,14},{7,15},{8,0},{9,1},... | collective-permute-start | bytes 1548296 | tf_op jit(solution)/shard_map/ppermute | solution.py:860
  196.7 16.5 %collective-permute-start.21 = (bf16[2,96,768]{2,1,0:T(8,128)(2,1)S(1)}, bf16[2,96,768]{2,1,0:T(8,128)(2,1)S(1)}, u32[]{:S(2)}, u32[]{:S(2)}) collective-permute-start(bf16[2,96,768]{2,1,0:T(8,128)(2,1)S(1)} %get-tuple-element.160), channel_id=1, source_target_pairs={{0,8},{1,9},{2,10},{3,11},{4,12},{5,13},{6,14},{7,15},{8,0},{9,1},... | collective-permute-start | bytes 884744 | tf_op jit(solution)/shard_map/ppermute | solution.py:860
  196.8 16.4 %collective-permute-start.22 = (bf16[2,96,768]{2,1,0:T(8,128)(2,1)S(1)}, bf16[2,96,768]{2,1,0:T(8,128)(2,1)S(1)}, u32[]{:S(2)}, u32[]{:S(2)}) collective-permute-start(bf16[2,96,768]{2,1,0:T(8,128)(2,1)S(1)} %get-tuple-element.169), channel_id=1, source_target_pairs={{0,4},{1,5},{2,6},{3,7},{4,0},{5,1},{6,2},{7,3},{8,12},{9,13},{10,... | collective-permute-start | bytes 884744 | tf_op jit(solution)/shard_map/ppermute | solution.py:860
  202.6 17.0 %collective-permute-start.25 = (bf16[4,96,384]{2,1,0:T(8,128)(2,1)S(1)}, bf16[4,96,384]{2,1,0:T(8,128)(2,1)S(1)}, u32[]{:S(2)}, u32[]{:S(2)}) collective-permute-start(bf16[4,96,384]{2,1,0:T(8,128)(2,1)S(1)} %get-tuple-element.166), channel_id=1, source_target_pairs={{0,4},{1,5},{2,6},{3,7},{4,0},{5,1},{6,2},{7,3},{8,12},{9,13},{10,... | collective-permute-start | bytes 884744 | tf_op jit(solution)/shard_map/ppermute | solution.py:860
  213.9 23.1 %collective-permute-start.29 = (bf16[2,96,768]{2,1,0:T(8,128)(2,1)S(1)}, bf16[2,96,768]{2,1,0:T(8,128)(2,1)S(1)}, u32[]{:S(2)}, u32[]{:S(2)}) collective-permute-start(bf16[2,96,768]{2,1,0:T(8,128)(2,1)S(1)} %get-tuple-element.170), channel_id=1, source_target_pairs={{0,16},{1,17},{2,18},{3,19},{4,20},{5,21},{6,22},{7,23},{8,24},{9,... | collective-permute-start | bytes 884744 | tf_op jit(solution)/shard_map/ppermute | solution.py:860
  216.6 17.6 %collective-permute-start.26 = (bf16[2,112,576]{2,1,0:T(8,128)(2,1)S(1)}, bf16[2,112,576]{2,1,0:T(8,128)(2,1)S(1)}, u32[]{:S(2)}, u32[]{:S(2)}) collective-permute-start(bf16[2,112,576]{2,1,0:T(8,128)(2,1)S(1)} %get-tuple-element.174), channel_id=1, source_target_pairs={{0,8},{1,9},{2,10},{3,11},{4,12},{5,13},{6,14},{7,15},{8,0},{9,1},... | collective-permute-start | bytes 774152 | tf_op jit(solution)/shard_map/ppermute | solution.py:860
  218.8 15.4 %collective-permute-start.27 = (bf16[2,112,576]{2,1,0:T(8,128)(2,1)S(1)}, bf16[2,112,576]{2,1,0:T(8,128)(2,1)S(1)}, u32[]{:S(2)}, u32[]{:S(2)}) collective-permute-start(bf16[2,112,576]{2,1,0:T(8,128)(2,1)S(1)} %get-tuple-element.181), channel_id=1, source_target_pairs={{0,4},{1,5},{2,6},{3,7},{4,0},{5,1},{6,2},{7,3},{8,12},{9,13},{10,... | collective-permute-start | bytes 774152 | tf_op jit(solution)/shard_map/ppermute | solution.py:860
  220.2 16.1 %collective-permute-start.28 = (bf16[2,96,384]{2,1,0:T(8,128)(2,1)S(1)}, bf16[2,96,384]{2,1,0:T(8,128)(2,1)S(1)}, u32[]{:S(2)}, u32[]{:S(2)}) collective-permute-start(bf16[2,96,384]{2,1,0:T(8,128)(2,1)S(1)} %get-tuple-element.176), channel_id=1, source_target_pairs={{0,8},{1,9},{2,10},{3,11},{4,12},{5,13},{6,14},{7,15},{8,0},{9,1},... | collective-permute-start | bytes 442376 | tf_op jit(solution)/shard_map/ppermute | solution.py:860
  234.9 11.3 %collective-permute-start.30 = (bf16[2,112,576]{2,1,0:T(8,128)(2,1)S(1)}, bf16[2,112,576]{2,1,0:T(8,128)(2,1)S(1)}, u32[]{:S(2)}, u32[]{:S(2)}) collective-permute-start(bf16[2,112,576]{2,1,0:T(8,128)(2,1)S(1)} %get-tuple-element.185), channel_id=1, source_target_pairs={{0,16},{1,17},{2,18},{3,19},{4,20},{5,21},{6,22},{7,23},{8,24},{9,... | collective-permute-start | bytes 774152 | tf_op jit(solution)/shard_map/ppermute | solution.py:860
  237.1 10.5 %collective-permute-start.33 = (bf16[2,96,768]{2,1,0:T(8,128)(2,1)S(1)}, bf16[2,96,768]{2,1,0:T(8,128)(2,1)S(1)}, u32[]{:S(2)}, u32[]{:S(2)}) collective-permute-start(bf16[2,96,768]{2,1,0:T(8,128)(2,1)S(1)} %shard_map.342.refs_0_), channel_id=1, source_target_pairs={{0,2},{1,3},{2,0},{3,1},{4,6},{5,7},{6,4},{7,5},{8,10},{9,11},{10,... | collective-permute-start | bytes 884744 | tf_op jit(solution)/shard_map/ppermute | solution.py:860
  (61 other events, 305.4 us)

commit v2 on v1

--- a/solution.py
+++ b/solution.py
@@ -817,7 +817,7 @@
 ORDER = ('dq', 'self', 'owner', 'ff1', 'kv0', 'rest1', 'kv1', 'ff2', 'kv2', 'ff3', 'rest2', 'kv3', 'memory', 'rest3', 'kv4', 'ff4', 'rest4', 'kv5', 'lay_ff', 'lay_rest', 'lay_kv')
 BEFORE = {'cross': ('early',), 'ffn': ('qc_z',), 'self': ('qc_y', 'do_stack'), 'ff1': ('exports',)}
 RELAY = ()
-COSTS = {'deal': 2, 'self_forward': 5, 'own_keys': 6, 'cross': 17, 'ffn': 12, 'dq': 20, 'self': 12, 'ff1': 5, 'rest1': 5, 'owner': 12, 'kv0': 7, 'memory': 6}
+COSTS = {'deal': 2, 'self_forward': 5, 'own_keys': 6, 'cross': 17, 'ffn': 12, 'dq': 20, 'self': 12, 'ff1': 3, 'rest1': 3, 'owner': 12, 'kv0': 3, 'memory': 3}
 LIMITS = {'self': 46}
 
 

time: 265 us -> 265 us (level)
  no operation moved by 1% of the time
where the time goes in v2:
time: 265 us; the launch traced here: 260 us
  Pallas kernels  76.4 us (29%)
  waiting for transfers between devices  63.4 us (24%)
  starting transfers between devices  44 us (17%)
  local copies, waits for them, and re-layouts  36.7 us (14%)
  blocking collectives  36.6 us (14%)
    pallas_call x26, Pallas kernels, local_kernel(): pl.pallas_call(body, out_shape=list(out_shape), in_specs=[pl.BlockSpec(me...  76.4 us
    ppermute x41, waiting for transfers between devices, hop(): return lax.ppermute(array, AXES, pairs)  63.4 us
    ppermute x41, starting transfers between devices, hop(): return lax.ppermute(array, AXES, pairs)  36.6 us
    unnamed x1, blocking collectives  36.6 us
    unnamed x105, local copies, waits for them, and re-layouts  31.4 us
    all_to_all x1, starting transfers between devices, fast_on_device(): lax.all_to_all(parcels_out, 'stream', split_axis=0, concat_axis=0, tiled=...  7.41 us
  transfers between devices with their start and end apart: 42, of which 14 were waited for; matrix products, arithmetic and copies ran while one was open for 3% of the time, Pallas kernels for 23%

profile of v2, /device:TPU:0, one launch (start us, length us, event | category | flops | bytes accessed | tf_op | source)
XLA Modules:
  0.0 260.3 jit_solution(1873660952483355471)
XLA Ops:
  5.2 7.4 %all-to-all-start = ((bf16[8,256,768]{2,1,0:T(8,128)(2,1)}), bf16[8,256,768]{2,1,0:T(8,128)(2,1)S(1)}, u32[]{:S(2)}, u32[]{:S(2)}) async-start(bf16[8,256,768]{2,1,0:T(8,128)(2,1)} %copy-done), calls=%async_computation | async-start | bytes 6291456 | tf_op jit(solution)/shard_map/all_to_all | solution.py:883
  12.7 2.0 copy-done.3
  17.2 3.0 %shard_map.323 = (bf16[128,2304]{1,0:T(8,128)(2,1)S(1)}, f32[128,768]{1,0:T(8,128)S(1)}, bf16[128,768]{1,0:T(8,128)(2,1)S(1)}, bf16[128,768]{1,0:T(8,128)(2,1)S(1)}, bf16[2304,128]{1,0:T(8,128)(2,1)}) custom-call(bf16[128,768]{1,0:T(8,128)(2,1)S(1)} %bitcast.47, bf16[768,2304]{1,0:T(8,128)(2,1)S(1)} %copy-done.3, bf16[768,768]{1,0:T(8,128)(2,1)S(1)} %copy-done.10, ...), custom_call_target="tpu_custom_call" | custom-call | flops 5750000128 | bytes 500000 | tf_op jit(solution)/shard_map/pallas_call | solution.py:338
  29.4 8.2 %collective-permute-done.1.refs_2_ = bf16[2304,128]{1,0:T(8,128)(2,1)} collective-permute-done((bf16[2304,128]{1,0:T(8,128)(2,1)}, bf16[2304,128]{1,0:T(8,128)(2,1)}, u32[]{:S(2)}, u32[]{:S(2)}) %collective-permute-start.1) | collective-permute-done | bytes 589856 | tf_op jit(solution)/shard_map/ppermute | solution.py:860
  40.7 2.6 %shard_map.324 = (bf16[1024,1536]{1,0:T(8,128)(2,1)S(1)}, bf16[768,1024]{1,0:T(8,128)(2,1)S(1)}) custom-call(bf16[1024,768]{1,0:T(8,128)(2,1)S(1)} %bitcast.46, bf16[768,1536]{1,0:T(8,128)(2,1)S(1)} %copy-done.4), custom_call_target="tpu_custom_call" | custom-call | flops 6899999744 | bytes 600000 | tf_op jit(solution)/shard_map/pallas_call | solution.py:338
  47.1 36.6 %all-reduce.1 = s32[64]{0:T(128)S(1)} all-reduce(s32[64]{0:T(128)S(1)} %dynamic-update-slice), channel_id=2, replica_groups=mesh['stream'=8,'rep'=4] {'stream'}, use_global_device_ids=true, to_apply=%add.1 | all-reduce | flops 64 | bytes 512
  83.8 2.8 %collective-permute-start.4 = (bf16[128,768]{1,0:T(8,128)(2,1)S(1)}, bf16[128,768]{1,0:T(8,128)(2,1)S(1)}, u32[]{:S(2)}, u32[]{:S(2)}) collective-permute-start(bf16[128,768]{1,0:T(8,128)(2,1)S(1)} %get-tuple-element.124.qc), channel_id=1, source_target_pairs={{0,16},{1,17},{2,18},{3,19},{4,20},{5,21},{6,22},{7,23},{8,24},{9,... | collective-permute-start | bytes 589832 | tf_op jit(solution)/shard_map/ppermute | solution.py:860
  89.8 11.1 %shard_map.325 = (bf16[128,768]{1,0:T(8,128)(2,1)S(1)}, bf16[2048,1536]{1,0:T(8,128)(2,1)S(1)}, f32[256,128]{1,0:T(8,128)S(1)}, f32[8,2048]{1,0:T(8,128)S(1)}) custom-call(s32[8,8]{1,0:T(8,128)S(1)} %reshape.89.routes_ref, s32[1]{0:T(128)} %bitcast.5.me_ref, bf16[128,768]{1,0:T(8,128)(2,1)S(1)} %get-tuple-element.124.qc, ...), custom_call_target="tpu_custom_call" | custom-call | flops 19549999104 | bytes 1700000 | tf_op jit(solution)/shard_map/pallas_call | solution.py:338
  101.1 2.3 copy-done.1
  103.4 2.3 copy-done.2
  105.7 7.5 %shard_map.326 = (bf16[128,768]{1,0:T(8,128)(2,1)}, f32[128,768]{1,0:T(8,128)S(1)}, bf16[144,768]{1,0:T(8,128)(2,1)S(1)}, f32[256,128]{1,0:T(8,128)S(1)}, f32[8,...) custom-call(s32[1]{0:T(128)} %bitcast.rep_ref, ...), custom_call_target="tpu_custom_call" | custom-call | flops 13799999488 | bytes 1200000 | tf_op jit(solution)/shard_map/pallas_call | solution.py:338
  113.2 2.3 collective-permute-start.9
  115.5 2.8 %collective-permute-start.8 = (bf16[144,768]{1,0:T(8,128)(2,1)S(1)}, bf16[144,768]{1,0:T(8,128)(2,1)S(1)}, u32[]{:S(2)}, u32[]{:S(2)}) collective-permute-start(bf16[144,768]{1,0:T(8,128)(2,1)S(1)} %get-tuple-element.125.do2), channel_id=1, source_target_pairs={{0,16},{1,17},{2,18},{3,19},{4,20},{5,21},{6,22},{7,23},{8,24},{9,... | collective-permute-start | bytes 663560 | tf_op jit(solution)/shard_map/ppermute | solution.py:860
  120.8 8.9 %shard_map.327.dqc_ref = bf16[128,768]{1,0:T(8,128)(2,1)S(1)} custom-call(bf16[128,768]{1,0:T(8,128)(2,1)S(1)} %get-tuple-element.124.qc, bf16[144,768]{1,0:T(8,128)(2,1)S(1)} %get-tuple-element.125.do2, bf16[2048,1536]{1,0:T(8,128)(2,1)S(1)} %get-tuple-element.126.kv, f32[8,2048]{1,0:T(8,128)S(1)} %get-tuple-element.127.bias_ref, ...), custom_call_target="tpu_custom_call" | custom-call | flops 23000000512 | bytes 2000000 | tf_op jit(solution)/shard_map/pallas_call | solution.py:338
  129.7 4.9 %collective-permute-done.8 = bf16[144,768]{1,0:T(8,128)(2,1)S(1)} collective-permute-done((bf16[144,768]{1,0:T(8,128)(2,1)S(1)}, bf16[144,768]{1,0:T(8,128)(2,1)S(1)}, u32[]{:S(2)}, u32[]{:S(2)}) %collective-permute-start.8) | collective-permute-done | bytes 221216 | tf_op jit(solution)/shard_map/ppermute | solution.py:860
  136.7 8.6 %shard_map.328 = (f32[128,768]{1,0:T(8,128)}, f32[8,768]{1,0:T(8,128)S(1)}, bf16[128,960]{1,0:T(8,128)(2,1)S(1)}, bf16[128,960]{1,0:T(8,128)(2,1)S(1)}, bf16[128...) custom-call(s32[1]{0:T(128)} %bitcast.rep_ref, bf16[128,768]{1,0:T(8,128)(2,1)S(1)} %shard_map.327.dqc_ref, ...), custom_call_target="tpu_custom_call" | custom-call | flops 13799999488 | bytes 1200000 | tf_op jit(solution)/shard_map/pallas_call | solution.py:338
  146.0 5.7 %collective-permute-done.15.refs_2_ = bf16[5760,128]{1,0:T(8,128)(2,1)S(1)} collective-permute-done((bf16[5760,128]{1,0:T(8,128)(2,1)S(1)}, bf16[5760,128]{1,0:T(8,128)(2,1)S(1)}, u32[]{:S(2)}, u32[]{:S(2)}) %collective-permute-start.15) | collective-permute-done | bytes 1474592 | tf_op jit(solution)/shard_map/ppermute | solution.py:860
  153.8 2.1 collective-permute-done.10.refs_3_
  155.9 11.4 %shard_map.329.dkv = bf16[1024,1536]{1,0:T(8,128)(2,1)S(1)} custom-call(s32[8]{0:T(128)S(1)} %broadcast_xor_fusion.where_ref, bf16[4,128,768]{2,1,0:T(8,128)(2,1)S(1)} %pad_maximum_fusion.1.refs_0_, bf16[4,128,768]{2,1,0:T(8,128)(2,1)S(1)} %collective-permute-done.6.refs_1_, bf16[4,144,768]{2,1,0:T(8,128)(2,1)S(1)} %pad_maximum_fusion.refs_2_, ...), custom_call_target="tpu_custom_call" | custom-call | flops 13799999488 | bytes 1200000 | tf_op jit(solution)/shard_map/pallas_call | solution.py:338
  167.4 2.6 %shard_map.330 = (bf16[4,96,768]{2,1,0:T(8,128)(2,1)S(1)}, bf16[4,96,768]{2,1,0:T(8,128)(2,1)S(1)}, bf16[4,96,768]{2,1,0:T(8,128)(2,1)S(1)}, bf16[4,96,768]{2,1,0:T(8,128)(2,1)S(1)}, bf16[768,192]{1,0:T(8,128)(2,1)S(1)}) custom-call(s32[3]{0:T(128)S(1)} %pad_add_fusion.bits_ref, bf16[4032,128]{1,0:T(8,128)(2,1)S(1)} %get-tuple-element.138.refs_0_, ...), custom_call_target="tpu_custom_call" | custom-call | flops 3449999872 | bytes 300000 | tf_op jit(solution)/shard_map/pallas_call | solution.py:338
  170.1 3.4 %shard_map.331 = (bf16[2,768,384]{2,1,0:T(8,128)(2,1)S(1)}, bf16[2,768,384]{2,1,0:T(8,128)(2,1)S(1)}) custom-call(s32[1]{0:T(128)} %bitcast.rep_ref, bf16[1024,1536]{1,0:T(8,128)(2,1)S(1)} %shard_map.329.dkv, bf16[768,1024]{1,0:T(8,128)(2,1)S(1)} %copy-done.31), custom_call_target="tpu_custom_call" | custom-call | flops 3449999872 | bytes 300000 | tf_op jit(solution)/shard_map/pallas_call | solution.py:338
  183.3 3.3 %shard_map.332 = (bf16[4,112,576]{2,1,0:T(8,128)(2,1)S(1)}, bf16[4,112,576]{2,1,0:T(8,128)(2,1)S(1)}, bf16[4,112,576]{2,1,0:T(8,128)(2,1)S(1)}, bf16[4,112,576]{2,1,0:T(8,128)(2,1)S(1)}) custom-call(s32[3]{0:T(128)S(1)} %pad_add_fusion.bits_ref, bf16[2304,128]{1,0:T(8,128)(2,1)} %get-tuple-element.147.refs_0_, ...), custom_call_target="tpu_custom_call" | custom-call | flops 3449999872 | bytes 300000 | tf_op jit(solution)/shard_map/pallas_call | solution.py:338
  189.8 4.3 %collective-permute-done.18.got0 = bf16[4,96,768]{2,1,0:T(8,128)(2,1)S(1)} collective-permute-done((bf16[4,96,768]{2,1,0:T(8,128)(2,1)}, bf16[4,96,768]{2,1,0:T(8,128)(2,1)S(1)}, u32[]{:S(2)}, u32[]{:S(2)}) %collective-permute-start.18) | collective-permute-done | bytes 589856 | tf_op jit(solution)/shard_map/ppermute | solution.py:860
  194.1 1.8 collective-permute-done.19.got1
  198.2 3.7 %collective-permute-done.20.got = bf16[768,384]{1,0:T(8,128)(2,1)S(1)} collective-permute-done((bf16[768,384]{1,0:T(8,128)(2,1)S(1)}, bf16[768,384]{1,0:T(8,128)(2,1)S(1)}, u32[]{:S(2)}, u32[]{:S(2)}) %collective-permute-start.20) | collective-permute-done | bytes 589856 | tf_op jit(solution)/shard_map/ppermute | solution.py:860
  203.9 9.4 %collective-permute-done.21.refs_1_ = bf16[2,96,768]{2,1,0:T(8,128)(2,1)S(1)} collective-permute-done((bf16[2,96,768]{2,1,0:T(8,128)(2,1)S(1)}, bf16[2,96,768]{2,1,0:T(8,128)(2,1)S(1)}, u32[]{:S(2)}, u32[]{:S(2)}) %collective-permute-start.21) | collective-permute-done | bytes 294944 | tf_op jit(solution)/shard_map/ppermute | solution.py:860
  213.9 1.9 collective-permute-start.29
  216.6 2.2 collective-permute-start.26
  221.4 3.8 %shard_map.339 = bf16[1024,768]{1,0:T(8,128)(2,1)} custom-call(bf16[1024,1536]{1,0:T(8,128)(2,1)S(1)} %copy-done.27, bf16[768,1536]{1,0:T(8,128)(2,1)S(1)} %copy-done.6), custom_call_target="tpu_custom_call" | custom-call | flops 3449999872 | bytes 300000 | tf_op jit(solution)/shard_map/pallas_call | solution.py:338
  225.2 9.0 %collective-permute-done.26.refs_1_ = bf16[2,112,576]{2,1,0:T(8,128)(2,1)S(1)} collective-permute-done((bf16[2,112,576]{2,1,0:T(8,128)(2,1)S(1)}, bf16[2,112,576]{2,1,0:T(8,128)(2,1)S(1)}, u32[]{:S(2)}, u32[]{:S(2)}) %collective-permute-start.26) | collective-permute-done | bytes 258080 | tf_op jit(solution)/shard_map/ppermute | solution.py:860
  239.2 7.0 %collective-permute-done.30.got = bf16[2,112,576]{2,1,0:T(8,128)(2,1)S(1)} collective-permute-done((bf16[2,112,576]{2,1,0:T(8,128)(2,1)S(1)}, bf16[2,112,576]{2,1,0:T(8,128)(2,1)S(1)}, u32[]{:S(2)}, u32[]{:S(2)}) %collective-permute-start.30) | collective-permute-done | bytes 258080 | tf_op jit(solution)/shard_map/ppermute | solution.py:860
  249.0 4.8 %collective-permute-done.36.refs_2_ = bf16[2,112,576]{2,1,0:T(8,128)(2,1)S(1)} collective-permute-done((bf16[2,112,576]{2,1,0:T(8,128)(2,1)S(1)}, bf16[2,112,576]{2,1,0:T(8,128)(2,1)S(1)}, u32[]{:S(2)}, u32[]{:S(2)}) %collective-permute-start.36) | collective-permute-done | bytes 258080 | tf_op jit(solution)/shard_map/ppermute | solution.py:860
  (210 shorter events, 68.2 us)
Async XLA Ops:
  5.2 78.5 %all-to-all-start = ((bf16[8,256,768]{2,1,0:T(8,128)(2,1)}), bf16[8,256,768]{2,1,0:T(8,128)(2,1)S(1)}, u32[]{:S(2)}, u32[]{:S(2)}) async-start(bf16[8,256,768]{2,1,0:T(8,128)(2,1)} %copy-done), calls=%async_computation | async-start | bytes 6291456 | tf_op jit(solution)/shard_map/all_to_all | solution.py:883
  22.5 15.1 %collective-permute-start.1 = (bf16[2304,128]{1,0:T(8,128)(2,1)}, bf16[2304,128]{1,0:T(8,128)(2,1)}, u32[]{:S(2)}, u32[]{:S(2)}) collective-permute-start(bf16[2304,128]{1,0:T(8,128)(2,1)} %get-tuple-element.147.refs_0_), channel_id=1, source_target_pairs={{0,2},{1,3},{2,0},{3,1},{4,6},{5,7},{6,4},{7,5},{8,10},{9,11},{10,... | collective-permute-start | bytes 1769480 | tf_op jit(solution)/shard_map/ppermute | solution.py:860
  24.0 22.1 %collective-permute-start = (bf16[2304,128]{1,0:T(8,128)(2,1)}, bf16[2304,128]{1,0:T(8,128)(2,1)}, u32[]{:S(2)}, u32[]{:S(2)}) collective-permute-start(bf16[2304,128]{1,0:T(8,128)(2,1)} %get-tuple-element.147.refs_0_), channel_id=1, source_target_pairs={{0,1},{1,0},{2,3},{3,2},{4,5},{5,4},{6,7},{7,6},{8,9},{9,8},{10,11... | collective-permute-start | bytes 1769480 | tf_op jit(solution)/shard_map/ppermute | solution.py:860
  83.8 17.2 %collective-permute-start.3 = (bf16[128,768]{1,0:T(8,128)(2,1)S(1)}, bf16[128,768]{1,0:T(8,128)(2,1)S(1)}, u32[]{:S(2)}, u32[]{:S(2)}) collective-permute-start(bf16[128,768]{1,0:T(8,128)(2,1)S(1)} %get-tuple-element.124.qc), channel_id=1, source_target_pairs={{0,8},{1,9},{2,10},{3,11},{4,12},{5,13},{6,14},{7,15},{8,0},{9,1},... | collective-permute-start | bytes 589832 | tf_op jit(solution)/shard_map/ppermute | solution.py:860
  83.8 17.2 %collective-permute-start.4 = (bf16[128,768]{1,0:T(8,128)(2,1)S(1)}, bf16[128,768]{1,0:T(8,128)(2,1)S(1)}, u32[]{:S(2)}, u32[]{:S(2)}) collective-permute-start(bf16[128,768]{1,0:T(8,128)(2,1)S(1)} %get-tuple-element.124.qc), channel_id=1, source_target_pairs={{0,16},{1,17},{2,18},{3,19},{4,20},{5,21},{6,22},{7,23},{8,24},{9,... | collective-permute-start | bytes 589832 | tf_op jit(solution)/shard_map/ppermute | solution.py:860
  86.6 14.4 %collective-permute-start.5 = (bf16[128,768]{1,0:T(8,128)(2,1)S(1)}, bf16[128,768]{1,0:T(8,128)(2,1)S(1)}, u32[]{:S(2)}, u32[]{:S(2)}) collective-permute-start(bf16[128,768]{1,0:T(8,128)(2,1)S(1)} %get-tuple-element.124.qc), channel_id=1, source_target_pairs={{0,24},{1,25},{2,26},{3,27},{4,28},{5,29},{6,30},{7,31},{8,16},{9,... | collective-permute-start | bytes 589832 | tf_op jit(solution)/shard_map/ppermute | solution.py:860
  113.2 16.5 %collective-permute-start.9 = (bf16[144,768]{1,0:T(8,128)(2,1)S(1)}, bf16[144,768]{1,0:T(8,128)(2,1)S(1)}, u32[]{:S(2)}, u32[]{:S(2)}) collective-permute-start(bf16[144,768]{1,0:T(8,128)(2,1)S(1)} %get-tuple-element.125.do2), channel_id=1, source_target_pairs={{0,24},{1,25},{2,26},{3,27},{4,28},{5,29},{6,30},{7,31},{8,16},{9,... | collective-permute-start | bytes 663560 | tf_op jit(solution)/shard_map/ppermute | solution.py:860
  115.5 19.1 %collective-permute-start.8 = (bf16[144,768]{1,0:T(8,128)(2,1)S(1)}, bf16[144,768]{1,0:T(8,128)(2,1)S(1)}, u32[]{:S(2)}, u32[]{:S(2)}) collective-permute-start(bf16[144,768]{1,0:T(8,128)(2,1)S(1)} %get-tuple-element.125.do2), channel_id=1, source_target_pairs={{0,16},{1,17},{2,18},{3,19},{4,20},{5,21},{6,22},{7,23},{8,24},{9,... | collective-permute-start | bytes 663560 | tf_op jit(solution)/shard_map/ppermute | solution.py:860
  118.3 16.3 %collective-permute-start.7 = (bf16[144,768]{1,0:T(8,128)(2,1)S(1)}, bf16[144,768]{1,0:T(8,128)(2,1)S(1)}, u32[]{:S(2)}, u32[]{:S(2)}) collective-permute-start(bf16[144,768]{1,0:T(8,128)(2,1)S(1)} %get-tuple-element.125.do2), channel_id=1, source_target_pairs={{0,8},{1,9},{2,10},{3,11},{4,12},{5,13},{6,14},{7,15},{8,0},{9,1},... | collective-permute-start | bytes 663560 | tf_op jit(solution)/shard_map/ppermute | solution.py:860
  118.5 18.1 %collective-permute-start.6 = (bf16[4,128,768]{2,1,0:T(8,128)(2,1)S(1)}, bf16[4,128,768]{2,1,0:T(8,128)(2,1)S(1)}, u32[]{:S(2)}, u32[]{:S(2)}) collective-permute-start(bf16[4,128,768]{2,1,0:T(8,128)(2,1)S(1)} %pad_maximum_fusion.1.refs_0_), channel_id=1, source_target_pairs={{0,4},{1,5},{2,6},{3,7},{4,0},{5,1},{6,2},{7,3},{8,12},{9,13},{10,... | collective-permute-start | bytes 2359304 | tf_op jit(solution)/shard_map/ppermute | solution.py:860
  119.3 32.5 %collective-permute-start.15 = (bf16[5760,128]{1,0:T(8,128)(2,1)S(1)}, bf16[5760,128]{1,0:T(8,128)(2,1)S(1)}, u32[]{:S(2)}, u32[]{:S(2)}) collective-permute-start(bf16[5760,128]{1,0:T(8,128)(2,1)S(1)} %get-tuple-element.139), channel_id=1, source_target_pairs={{0,2},{1,3},{2,0},{3,1},{4,6},{5,7},{6,4},{7,5},{8,10},{9,11},{10,... | collective-permute-start | bytes 4423688 | tf_op jit(solution)/shard_map/ppermute | solution.py:860
  134.8 21.1 %collective-permute-start.10 = (bf16[4,144,768]{2,1,0:T(8,128)(2,1)S(1)}, bf16[4,144,768]{2,1,0:T(8,128)(2,1)S(1)}, u32[]{:S(2)}, u32[]{:S(2)}) collective-permute-start(bf16[4,144,768]{2,1,0:T(8,128)(2,1)S(1)} %pad_maximum_fusion.refs_2_), channel_id=1, source_target_pairs={{0,4},{1,5},{2,6},{3,7},{4,0},{5,1},{6,2},{7,3},{8,12},{9,13},{10,... | collective-permute-start | bytes 2654216 | tf_op jit(solution)/shard_map/ppermute | solution.py:860
  151.7 15.6 %collective-permute-start.16 = (bf16[5760,128]{1,0:T(8,128)(2,1)S(1)}, bf16[5760,128]{1,0:T(8,128)(2,1)S(1)}, u32[]{:S(2)}, u32[]{:S(2)}) collective-permute-start(bf16[5760,128]{1,0:T(8,128)(2,1)S(1)} %collective-permute-done.15.refs_2_), channel_id=1, source_target_pairs={{0,1},{1,0},{2,3},{3,2},{4,5},{5,4},{6,7},{7,6},{8,9},{9,8},{10,11... | collective-permute-start | bytes 4423688 | tf_op jit(solution)/shard_map/ppermute | solution.py:860
  151.8 15.6 %collective-permute-start.14 = (bf16[4032,128]{1,0:T(8,128)(2,1)S(1)}, bf16[4032,128]{1,0:T(8,128)(2,1)S(1)}, u32[]{:S(2)}, u32[]{:S(2)}) collective-permute-start(bf16[4032,128]{1,0:T(8,128)(2,1)S(1)} %get-tuple-element.138.refs_0_), channel_id=1, source_target_pairs={{0,1},{1,0},{2,3},{3,2},{4,5},{5,4},{6,7},{7,6},{8,9},{9,8},{10,11... | collective-permute-start | bytes 3096584 | tf_op jit(solution)/shard_map/ppermute | solution.py:860
  152.3 15.0 %collective-permute-start.11 = (bf16[128,960]{1,0:T(8,128)(2,1)S(1)}, bf16[128,960]{1,0:T(8,128)(2,1)S(1)}, u32[]{:S(2)}, u32[]{:S(2)}) collective-permute-start(bf16[128,960]{1,0:T(8,128)(2,1)S(1)} %get-tuple-element.135), channel_id=1, source_target_pairs={{0,1},{1,0},{2,3},{3,2},{4,5},{5,4},{6,7},{7,6},{8,9},{9,8},{10,11... | collective-permute-start | bytes 737288 | tf_op jit(solution)/shard_map/ppermute | solution.py:860
  152.3 15.0 %collective-permute-start.12 = (bf16[128,960]{1,0:T(8,128)(2,1)S(1)}, bf16[128,960]{1,0:T(8,128)(2,1)S(1)}, u32[]{:S(2)}, u32[]{:S(2)}) collective-permute-start(bf16[128,960]{1,0:T(8,128)(2,1)S(1)} %get-tuple-element.136), channel_id=1, source_target_pairs={{0,2},{1,3},{2,0},{3,1},{4,6},{5,7},{6,4},{7,5},{8,10},{9,11},{10,... | collective-permute-start | bytes 737288 | tf_op jit(solution)/shard_map/ppermute | solution.py:860
  155.9 11.4 %collective-permute-start.13 = (bf16[128,960]{1,0:T(8,128)(2,1)S(1)}, bf16[128,960]{1,0:T(8,128)(2,1)S(1)}, u32[]{:S(2)}, u32[]{:S(2)}) collective-permute-start(bf16[128,960]{1,0:T(8,128)(2,1)S(1)} %get-tuple-element.137), channel_id=1, source_target_pairs={{0,3},{1,2},{2,1},{3,0},{4,7},{5,6},{6,5},{7,4},{8,11},{9,10},{10,... | collective-permute-start | bytes 737288 | tf_op jit(solution)/shard_map/ppermute | solution.py:860
  174.6 12.1 %collective-permute-start.17 = (bf16[2,768,384]{2,1,0:T(8,128)(2,1)S(1)}, bf16[2,768,384]{2,1,0:T(8,128)(2,1)S(1)}, u32[]{:S(2)}, u32[]{:S(2)}) collective-permute-start(bf16[2,768,384]{2,1,0:T(8,128)(2,1)S(1)} %get-tuple-element.154), channel_id=1, source_target_pairs={{0,1},{1,0},{2,3},{3,2},{4,5},{5,4},{6,7},{7,6},{8,9},{9,8},{10,11... | collective-permute-start | bytes 3538952 | tf_op jit(solution)/shard_map/ppermute | solution.py:860
  177.7 16.4 %collective-permute-start.18 = (bf16[4,96,768]{2,1,0:T(8,128)(2,1)}, bf16[4,96,768]{2,1,0:T(8,128)(2,1)S(1)}, u32[]{:S(2)}, u32[]{:S(2)}) collective-permute-start(bf16[4,96,768]{2,1,0:T(8,128)(2,1)} %copy-done.17), channel_id=1, source_target_pairs={{0,4},{1,5},{2,6},{3,7},{4,0},{5,1},{6,2},{7,3},{8,12},{9,13},{10,... | collective-permute-start | bytes 1769480 | tf_op jit(solution)/shard_map/ppermute | solution.py:860
  179.4 16.4 %collective-permute-start.19 = (bf16[4,96,768]{2,1,0:T(8,128)(2,1)}, bf16[4,96,768]{2,1,0:T(8,128)(2,1)S(1)}, u32[]{:S(2)}, u32[]{:S(2)}) collective-permute-start(bf16[4,96,768]{2,1,0:T(8,128)(2,1)} %copy-done.16), channel_id=1, source_target_pairs={{0,8},{1,9},{2,10},{3,11},{4,12},{5,13},{6,14},{7,15},{8,0},{9,1},... | collective-permute-start | bytes 1769480 | tf_op jit(solution)/shard_map/ppermute | solution.py:860
  187.0 15.0 %collective-permute-start.20 = (bf16[768,384]{1,0:T(8,128)(2,1)S(1)}, bf16[768,384]{1,0:T(8,128)(2,1)S(1)}, u32[]{:S(2)}, u32[]{:S(2)}) collective-permute-start(bf16[768,384]{1,0:T(8,128)(2,1)S(1)} %get-tuple-element.162), channel_id=1, source_target_pairs={{0,2},{1,3},{2,0},{3,1},{4,6},{5,7},{6,4},{7,5},{8,10},{9,11},{10,... | collective-permute-start | bytes 1769480 | tf_op jit(solution)/shard_map/ppermute | solution.py:860
  187.6 28.2 %collective-permute-start.23 = (bf16[4,112,576]{2,1,0:T(8,128)(2,1)S(1)}, bf16[4,112,576]{2,1,0:T(8,128)(2,1)S(1)}, u32[]{:S(2)}, u32[]{:S(2)}) collective-permute-start(bf16[4,112,576]{2,1,0:T(8,128)(2,1)S(1)} %get-tuple-element.152), channel_id=1, source_target_pairs={{0,4},{1,5},{2,6},{3,7},{4,0},{5,1},{6,2},{7,3},{8,12},{9,13},{10,... | collective-permute-start | bytes 1548296 | tf_op jit(solution)/shard_map/ppermute | solution.py:860
  189.0 26.8 %collective-permute-start.24 = (bf16[4,112,576]{2,1,0:T(8,128)(2,1)S(1)}, bf16[4,112,576]{2,1,0:T(8,128)(2,1)S(1)}, u32[]{:S(2)}, u32[]{:S(2)}) collective-permute-start(bf16[4,112,576]{2,1,0:T(8,128)(2,1)S(1)} %get-tuple-element.173), channel_id=1, source_target_pairs={{0,8},{1,9},{2,10},{3,11},{4,12},{5,13},{6,14},{7,15},{8,0},{9,1},... | collective-permute-start | bytes 1548296 | tf_op jit(solution)/shard_map/ppermute | solution.py:860
  196.7 16.5 %collective-permute-start.21 = (bf16[2,96,768]{2,1,0:T(8,128)(2,1)S(1)}, bf16[2,96,768]{2,1,0:T(8,128)(2,1)S(1)}, u32[]{:S(2)}, u32[]{:S(2)}) collective-permute-start(bf16[2,96,768]{2,1,0:T(8,128)(2,1)S(1)} %get-tuple-element.160), channel_id=1, source_target_pairs={{0,8},{1,9},{2,10},{3,11},{4,12},{5,13},{6,14},{7,15},{8,0},{9,1},... | collective-permute-start | bytes 884744 | tf_op jit(solution)/shard_map/ppermute | solution.py:860
  196.8 16.4 %collective-permute-start.22 = (bf16[2,96,768]{2,1,0:T(8,128)(2,1)S(1)}, bf16[2,96,768]{2,1,0:T(8,128)(2,1)S(1)}, u32[]{:S(2)}, u32[]{:S(2)}) collective-permute-start(bf16[2,96,768]{2,1,0:T(8,128)(2,1)S(1)} %get-tuple-element.169), channel_id=1, source_target_pairs={{0,4},{1,5},{2,6},{3,7},{4,0},{5,1},{6,2},{7,3},{8,12},{9,13},{10,... | collective-permute-start | bytes 884744 | tf_op jit(solution)/shard_map/ppermute | solution.py:860
  202.6 17.0 %collective-permute-start.25 = (bf16[4,96,384]{2,1,0:T(8,128)(2,1)S(1)}, bf16[4,96,384]{2,1,0:T(8,128)(2,1)S(1)}, u32[]{:S(2)}, u32[]{:S(2)}) collective-permute-start(bf16[4,96,384]{2,1,0:T(8,128)(2,1)S(1)} %get-tuple-element.166), channel_id=1, source_target_pairs={{0,4},{1,5},{2,6},{3,7},{4,0},{5,1},{6,2},{7,3},{8,12},{9,13},{10,... | collective-permute-start | bytes 884744 | tf_op jit(solution)/shard_map/ppermute | solution.py:860
  213.9 23.1 %collective-permute-start.29 = (bf16[2,96,768]{2,1,0:T(8,128)(2,1)S(1)}, bf16[2,96,768]{2,1,0:T(8,128)(2,1)S(1)}, u32[]{:S(2)}, u32[]{:S(2)}) collective-permute-start(bf16[2,96,768]{2,1,0:T(8,128)(2,1)S(1)} %get-tuple-element.170), channel_id=1, source_target_pairs={{0,16},{1,17},{2,18},{3,19},{4,20},{5,21},{6,22},{7,23},{8,24},{9,... | collective-permute-start | bytes 884744 | tf_op jit(solution)/shard_map/ppermute | solution.py:860
  216.6 17.6 %collective-permute-start.26 = (bf16[2,112,576]{2,1,0:T(8,128)(2,1)S(1)}, bf16[2,112,576]{2,1,0:T(8,128)(2,1)S(1)}, u32[]{:S(2)}, u32[]{:S(2)}) collective-permute-start(bf16[2,112,576]{2,1,0:T(8,128)(2,1)S(1)} %get-tuple-element.174), channel_id=1, source_target_pairs={{0,8},{1,9},{2,10},{3,11},{4,12},{5,13},{6,14},{7,15},{8,0},{9,1},... | collective-permute-start | bytes 774152 | tf_op jit(solution)/shard_map/ppermute | solution.py:860
  218.8 15.4 %collective-permute-start.27 = (bf16[2,112,576]{2,1,0:T(8,128)(2,1)S(1)}, bf16[2,112,576]{2,1,0:T(8,128)(2,1)S(1)}, u32[]{:S(2)}, u32[]{:S(2)}) collective-permute-start(bf16[2,112,576]{2,1,0:T(8,128)(2,1)S(1)} %get-tuple-element.181), channel_id=1, source_target_pairs={{0,4},{1,5},{2,6},{3,7},{4,0},{5,1},{6,2},{7,3},{8,12},{9,13},{10,... | collective-permute-start | bytes 774152 | tf_op jit(solution)/shard_map/ppermute | solution.py:860
  220.2 16.1 %collective-permute-start.28 = (bf16[2,96,384]{2,1,0:T(8,128)(2,1)S(1)}, bf16[2,96,384]{2,1,0:T(8,128)(2,1)S(1)}, u32[]{:S(2)}, u32[]{:S(2)}) collective-permute-start(bf16[2,96,384]{2,1,0:T(8,128)(2,1)S(1)} %get-tuple-element.176), channel_id=1, source_target_pairs={{0,8},{1,9},{2,10},{3,11},{4,12},{5,13},{6,14},{7,15},{8,0},{9,1},... | collective-permute-start | bytes 442376 | tf_op jit(solution)/shard_map/ppermute | solution.py:860
  234.9 11.3 %collective-permute-start.30 = (bf16[2,112,576]{2,1,0:T(8,128)(2,1)S(1)}, bf16[2,112,576]{2,1,0:T(8,128)(2,1)S(1)}, u32[]{:S(2)}, u32[]{:S(2)}) collective-permute-start(bf16[2,112,576]{2,1,0:T(8,128)(2,1)S(1)} %get-tuple-element.185), channel_id=1, source_target_pairs={{0,16},{1,17},{2,18},{3,19},{4,20},{5,21},{6,22},{7,23},{8,24},{9,... | collective-permute-start | bytes 774152 | tf_op jit(solution)/shard_map/ppermute | solution.py:860
  237.1 10.5 %collective-permute-start.33 = (bf16[2,96,768]{2,1,0:T(8,128)(2,1)S(1)}, bf16[2,96,768]{2,1,0:T(8,128)(2,1)S(1)}, u32[]{:S(2)}, u32[]{:S(2)}) collective-permute-start(bf16[2,96,768]{2,1,0:T(8,128)(2,1)S(1)} %shard_map.342.refs_0_), channel_id=1, source_target_pairs={{0,2},{1,3},{2,0},{3,1},{4,6},{5,7},{6,4},{7,5},{8,10},{9,11},{10,... | collective-permute-start | bytes 884744 | tf_op jit(solution)/shard_map/ppermute | solution.py:860
  (61 other events, 305.4 us)
